TPU v7x, 256 devices: a whole 4x4x8 slice. The times are simulated.
256 devices in a mesh: fsdp: 16 (over z_lo, y), seq: 16 (over z_hi, x, core).
Axes of the slice: x: 4, y: 4, z: 8 (z_hi: 2, z_lo: 4; z = z_hi * 4 + z_lo), core: 2. Of those that a mesh axis runs over, the one named last changes fastest.
Arguments:
- queries: bfloat16 [32768, 4096], P(('fsdp', 'seq')), may hold values from -6 to 6
- keys: bfloat16 [32768, 4096], P(('fsdp', 'seq')), may hold values from -6 to 6
- values: bfloat16 [32768, 4096], P(('fsdp', 'seq')), may hold values from -6 to 6
- cotangent: bfloat16 [32768, 4096], P(('fsdp', 'seq')), may hold values from -24 to 24
- out_weight: bfloat16 [4096, 4096], P('seq', 'fsdp'), may hold values from -0.09375 to 0.09375
- short_taps: float32 [3, 7, 4096], P(None, None, 'seq'), may hold values from -2 to 2
- long_taps: float32 [128, 256], P(None, 'seq'), may hold values from -0.5 to 0.5
- skip_gain: float32 [4096], P('seq'), may hold values from -1 to 1
Outputs:
- query_grad: bfloat16 [32768, 4096], P(('fsdp', 'seq'))
- key_grad: bfloat16 [32768, 4096], P(('fsdp', 'seq'))
- value_grad: bfloat16 [32768, 4096], P(('fsdp', 'seq'))
- weight_grad: float32 [4096, 4096], P('seq', 'fsdp')
- short_grad: float32 [3, 7, 4096], P(None, None, 'seq')
- long_grad: float32 [128, 256], P(None, 'seq')
- gain_grad: float32 [4096], P('seq')
All inputs are finite; a program needn't handle non-finite values.
Results may differ from a plain program's by a relative error of at most 0.0075.
Values may be sent and summed in bfloat16 or wider, within the bound.
A program may use at most 256 MiB of HBM per device.

v0:
```python
import jax
import jax.numpy as jnp
from jax import lax
from jax.sharding import PartitionSpec as P

SHORT = 7
LTAPS = 128


precise = lax.Precision.HIGHEST


def from_behind(block, axis, distance):
    devices = range(lax.axis_size(axis))
    route = [(i - distance, i) for i in devices if i - distance in devices]
    return lax.ppermute(block, axis, route)


def make_tables(taps):
    taps_count = taps.shape[0]
    lag_rows = jnp.arange(taps_count)[:, None] - jnp.arange(taps_count)[None, :]
    tap_ids = jnp.arange(taps_count)
    near_pick = (lag_rows[:, :, None] == tap_ids[None, None, :]).astype(jnp.float32)
    far_pick = ((lag_rows + taps_count)[:, :, None] == tap_ids[None, None, :]).astype(jnp.float32)
    near_taps = jnp.einsum("tsj,jg->gts", near_pick, taps, precision=precise)
    far_taps = jnp.einsum("tsj,jg->gts", far_pick, taps, precision=precise)
    return (near_pick, far_pick, near_taps, far_taps)


def to_blocks(field, block_len, group_count):
    row_count, col_count = field.shape
    return field.reshape(row_count // block_len, block_len, group_count, col_count // group_count)


def long_forward(product, edge_rows, tables):
    near_taps, far_taps = (tables[2], tables[3])
    group_count, block_len = (near_taps.shape[0], near_taps.shape[1])
    row_count, col_count = product.shape
    current = to_blocks(product, block_len, group_count)
    earlier = to_blocks(
        jnp.concatenate([edge_rows, product[: row_count - block_len]], 0), block_len, group_count
    )
    total = jnp.einsum("gts,bsgc->btgc", near_taps, current, precision=precise)
    total = total + jnp.einsum("gts,bsgc->btgc", far_taps, earlier, precision=precise)
    return total.reshape(row_count, col_count)


def long_backward(slope_grad, next_rows, product, edge_rows, tables):
    near_pick, far_pick, near_taps, far_taps = tables
    group_count, block_len = (near_taps.shape[0], near_taps.shape[1])
    row_count, col_count = product.shape
    current_d = to_blocks(slope_grad, block_len, group_count)
    later_d = to_blocks(
        jnp.concatenate([slope_grad[block_len:], next_rows], 0), block_len, group_count
    )
    product_grad = jnp.einsum("gts,btgc->bsgc", near_taps, current_d, precision=precise)
    product_grad = product_grad + jnp.einsum("gts,btgc->bsgc", far_taps, later_d, precision=precise)
    current_z = to_blocks(product, block_len, group_count)
    earlier_z = to_blocks(
        jnp.concatenate([edge_rows, product[: row_count - block_len]], 0), block_len, group_count
    )
    gram_near = jnp.einsum("btgc,bsgc->gts", current_d, current_z, precision=precise)
    gram_far = jnp.einsum("btgc,bsgc->gts", current_d, earlier_z, precision=precise)
    taps_grad = jnp.einsum("tsj,gts->jg", near_pick, gram_near, precision=precise)
    taps_grad = taps_grad + jnp.einsum("tsj,gts->jg", far_pick, gram_far, precision=precise)
    return (product_grad.reshape(row_count, col_count), taps_grad)


def short_forward(inputs_f, edge_rows, taps):
    tap_count = taps.shape[1]
    row_count = inputs_f.shape[1]
    extended = jnp.concatenate([edge_rows, inputs_f], 1)
    result = jnp.zeros(inputs_f.shape, jnp.float32)
    for offset in range(tap_count):
        begin = tap_count - 1 - offset
        result = result + taps[:, offset, None, :] * extended[:, begin : begin + row_count]
    return result


def short_backward(feat_grad, next_rows, inputs_f, edge_rows, taps):
    tap_count = taps.shape[1]
    row_count = inputs_f.shape[1]
    later = jnp.concatenate([feat_grad, next_rows], 1)
    extended = jnp.concatenate([edge_rows, inputs_f], 1)
    inputs_grad = jnp.zeros(inputs_f.shape, jnp.float32)
    taps_list = []
    for offset in range(tap_count):
        inputs_grad = inputs_grad + taps[:, offset, None, :] * later[:, offset : offset + row_count]
        begin = tap_count - 1 - offset
        taps_list.append(jnp.sum(feat_grad * extended[:, begin : begin + row_count], axis=1))
    return (inputs_grad, jnp.stack(taps_list, axis=1))


def gate_forward(inputs_b, edge_in, taps_short):
    features = short_forward(inputs_b.astype(jnp.float32), edge_in.astype(jnp.float32), taps_short)
    return (features, features[1] * features[2])


def cotangent_terms(cotangent, mixed_groups, full_cols):
    all_rows = lax.all_gather(cotangent, "seq", axis=0, tiled=True)
    mixed_grad = lax.dot_general(
        all_rows, full_cols, (((1,), (1,)), ((), ())), preferred_element_type=jnp.float32
    )
    weight_sum = lax.dot_general(
        mixed_groups, all_rows, (((0,), (0,)), ((), ())), preferred_element_type=jnp.float32
    )
    weight_part = lax.psum_scatter(weight_sum, "fsdp", scatter_dimension=1, tiled=True)
    return (mixed_grad, weight_part)


def body(queries, keys, values, cotangent, out_weight, short_taps, long_taps, skip_gain):
    tok_rows = queries.shape[0]
    grad_scale = float(tok_rows * lax.axis_size("fsdp") * lax.axis_size("seq")) ** (-0.5)
    stacked = jnp.stack([queries, keys, values])
    full_cols = lax.all_gather(out_weight, "fsdp", axis=1, tiled=True)
    grouped = lax.all_to_all(stacked, "seq", split_axis=2, concat_axis=1, tiled=True)
    group_rows = grouped.shape[1]
    edge_in = from_behind(grouped[:, group_rows - (SHORT - 1) :], "fsdp", 1)
    features, product = gate_forward(grouped, edge_in, short_taps)
    edge_prod = from_behind(product[group_rows - LTAPS :].astype(jnp.bfloat16), "fsdp", 1).astype(
        jnp.float32
    )
    tables = make_tables(long_taps)
    filtered = long_forward(product, edge_prod, tables) + skip_gain * product
    mixed_out = (features[0] * filtered).astype(jnp.bfloat16)
    mixed_grad, weight_part = cotangent_terms(cotangent, mixed_out, full_cols)
    query_feat = mixed_grad * filtered
    slope_grad = mixed_grad * features[0]
    next_slope = from_behind(slope_grad[:LTAPS].astype(jnp.bfloat16), "fsdp", -1).astype(
        jnp.float32
    )
    product_core, long_part = long_backward(slope_grad, next_slope, product, edge_prod, tables)
    product_grad = product_core + skip_gain * slope_grad
    gain_part = jnp.sum(slope_grad * product, axis=0)
    feat_grad = jnp.stack([query_feat, product_grad * features[2], product_grad * features[1]])
    next_feat = from_behind(feat_grad[:, : SHORT - 1], "fsdp", -1)
    inputs_grad, short_part = short_backward(
        feat_grad, next_feat, grouped.astype(jnp.float32), edge_in.astype(jnp.float32), short_taps
    )
    token_grads = lax.all_to_all(
        inputs_grad.astype(jnp.bfloat16), "seq", split_axis=1, concat_axis=2, tiled=True
    )
    short_sum, long_sum, gain_sum = lax.psum((short_part, long_part, gain_part), "fsdp")
    return (
        token_grads[0],
        token_grads[1],
        token_grads[2],
        weight_part * grad_scale,
        short_sum * grad_scale,
        long_sum * grad_scale,
        gain_sum * grad_scale,
    )


def solution(mesh):
    return jax.shard_map(
        body,
        mesh=mesh,
        in_specs=(
            P(("fsdp", "seq"), None),
            P(("fsdp", "seq"), None),
            P(("fsdp", "seq"), None),
            P(("fsdp", "seq"), None),
            P("seq", "fsdp"),
            P(None, None, "seq"),
            P(None, "seq"),
            P("seq"),
        ),
        out_specs=(
            P(("fsdp", "seq"), None),
            P(("fsdp", "seq"), None),
            P(("fsdp", "seq"), None),
            P("seq", "fsdp"),
            P(None, None, "seq"),
            P(None, "seq"),
            P("seq"),
        ),
        check_vma=False,
    )
```

profile of v0, /device:TPU:2, one launch (start us, length us, event | category | flops | bytes accessed | tf_op | source)
XLA Modules:
  0.0 667.5 jit_solution(1114205000243679570)
XLA Ops:
  8.7 2.2 pad_maximum_fusion.3
  10.9 4.8 copy.83
  15.6 11.6 %all-to-all-start = ((bf16[3,128,4096]{1,0,2:T(4,128)(2,1)}), bf16[3,128,4096]{1,0,2:T(4,128)(2,1)}, u32[]{:S(2)}, u32[]{:S(2)}) async-start(bf16[3,128,4096]{1,0,2:T(4,128)(2,1)} %copy.83), calls=%async_computation | async-start | bytes 8388608 | tf_op jit(solution)/shard_map/all_to_all | solution.py:116
  27.4 2.8 iota_compare_fusion
  30.2 5.8 fusion.33
  36.0 2.8 iota_compare_fusion.1
  38.8 5.8 fusion.30
  44.5 74.0 %all-to-all-done = bf16[3,128,4096]{1,0,2:T(4,128)(2,1)} async-done(((bf16[3,128,4096]{1,0,2:T(4,128)(2,1)}), bf16[3,128,4096]{1,0,2:T(4,128)(2,1)}, u32[]{:S(2)}, u32[]{:S(2)}) %all-to-all-start) | async-done | bytes 3145760 | tf_op jit(solution)/shard_map/all_to_all | solution.py:116
  118.5 5.5 copy.84
  124.0 1.8 collective-permute-start
  126.7 2.5 copy-done.8
  129.2 6.6 multiply_add_fusion
  135.8 179.3 %all-gather.3.cloned.1.call-done = bf16[2048,4096]{1,0:T(8,128)(2,1)} async-done(((bf16[128,4096]{1,0:T(8,128)(2,1)}), bf16[2048,4096]{1,0:T(8,128)(2,1)}) %all-gather.3.cloned.1.call-update) | async-done | bytes 16777232 | tf_op jit(solution)/shard_map/all_gather | solution.py:100
  315.1 16.0 %multiply_reduce_fusion.6 = (f32[256]{0:T(256)S(1)}, f32[2048,256]{1,0:T(8,128)S(1)}, f32[2048,256]{1,0:T(8,128)}, f32[2048,256]{1,0:T(8,128)}) fusion(f32[3,2048,256]{2,1,0:T(8,128)} %multiply_add_fusion, bf16[2048,4096]{1,0:T(8,128)(2,1)} %all-gather.3.cloned.1.call-done, bf16[256,4096]{1,0:T(8,128)(2,1)} %all-gather.5.cloned.1.call-done), kind=kOutput, calls=%fused_computation.58 | convolution fusion | flops 4297064448 | bytes 31458304 | tf_op jit(solution)/shard_map/dot_general | solution.py:101
  331.1 3.4 collective-permute-start.1
  336.1 2.9 copy.85
  339.0 3.3 copy.131
  343.7 3.0 copy.95
  352.3 1.8 copy.89
  354.1 2.1 copy.132
  356.3 2.9 fusion.21
  359.2 2.9 add_bitcast_fusion.1
  362.8 2.3 copy.178
  365.0 1.9 copy.94
  367.0 3.1 pad_maximum_fusion.5
  370.0 3.1 copy.98
  373.1 2.1 copy.135
  375.3 2.9 fusion.17
  378.2 2.9 add_bitcast_fusion
  381.8 2.2 copy.177
  383.9 2.9 copy.102
  386.9 5.9 bitcast_multiply_fusion
  395.6 1.7 collective-permute-start.3
  397.3 13.4 %fusion.37 = f32[256,4096]{1,0:T(8,128)} fusion(bf16[2048,4096]{1,0:T(8,128)(2,1)} %all-gather.3.cloned.1.call-done, f32[3,2048,256]{2,1,0:T(8,128)} %multiply_add_fusion, f32[2048,256]{1,0:T(8,128)S(1)} %copy.94, f32[2048,256]{1,0:T(8,128)S(1)} %copy-done.12, f32[256]{0:T(256)S(1)} %copy-done.24), kind=kOutput, calls=%fused_computation.73 | convolution fusion | flops 4297064448 | bytes 27264000 | tf_op jit(solution)/shard_map/dot_general | solution.py:104
  410.7 3.1 pad_maximum_fusion
  413.8 7.9 %fusion.10 = bf16[3,2048,256]{2,1,0:T(8,128)(2,1)} fusion(f32[3,2054,256]{2,1,0:T(8,128)S(1)} %pad_maximum_fusion, f32[3,256]{1,0:T(4,128)S(1)} %get-tuple-element.57, f32[3,256]{1,0:T(4,128)S(1)} %get-tuple-element.58, f32[3,256]{1,0:T(4,128)S(1)} %get-tuple-element.59, f32[3,256]{1,0:T(4,128)S(1)} %get-tuple-element.60, ...), kind=kLoop, calls=%fused_computation.19 | loop fusion | flops 25165824 | bytes 47207424 | tf_op jit(solution)/shard_map/convert_element_type | solution.py:141
  421.7 6.8 %copy.103 = bf16[3,2048,256]{2,0,1:T(4,128)(2,1)} copy(bf16[3,2048,256]{2,1,0:T(8,128)(2,1)} %fusion.10) | data formatting | bytes 6291456 | tf_op jit(solution)/shard_map/convert_element_type | solution.py:141
  428.5 6.6 all-to-all-start.1
  435.1 5.2 convolution_bitcast_fusion.1
  440.9 3.4 convolution_bitcast_fusion.3
  444.3 6.9 %convolution_bitcast_fusion = f32[16,128,128]{2,1,0:T(8,128)} fusion(f32[16,128,16,16]{1,0,3,2:T(8,128)} %bitcast.163, f32[16,128,16,16]{1,0,3,2:T(8,128)} %bitcast.169), kind=kOutput, calls=%fused_computation.68 | convolution fusion | flops 805306368 | bytes 5242880 | tf_op jit(solution)/shard_map/btgc,bsgc->gts/dot_general | solution.py:63
  451.2 1.7 copy.108
  452.9 3.8 fusion.16
  457.4 15.6 %multiply_reduce_fusion.1 = (f32[3,256]{1,0:T(4,128)S(1)}, f32[3,256]{1,0:T(4,128)S(1)}, f32[3,256]{1,0:T(4,128)S(1)}, f32[3,256]{1,0:T(4,128)S(1)}, f32[3,256]{1,0:T(4,128)S(1)}, /*index=5*/f32[3,256]{1,0:T(4,128)S(1)}) fusion(f32[3,2048,256]{2,1,0:T(8,128)} %copy-done.8, f32[3,6,256]{2,1,0:T(8,128)S(1)} %convert_element_type.28, ...), kind=kLoop, calls=%fused_computation.35 | loop fusion | flops 31452672 | bytes 12619776 | tf_op jit(solution)/shard_map/reduce_sum | solution.py:90
  473.1 3.4 fusion.36
  476.5 163.1 %all-reduce = (f32[3,7,256]{2,0,1:T(4,128)S(1)}, f32[128,16]{0,1:T(8,128)S(1)}, f32[256]{0:T(256)S(1)}) all-reduce(f32[3,7,256]{2,0,1:T(4,128)S(1)} %constant_dynamic-update-slice_fusion, f32[128,16]{0,1:T(8,128)S(1)} %fusion.36, f32[256]{0:T(256)S(1)} %get-tuple-element.37), channel_id=1, replica_groups=mesh['fsdp'=16,'seq'=16] {'fsdp'}, use_global_device_ids=true, to_apply=%region_8.0 | all-reduce | flops 7680 | bytes 61440 | tf_op jit(solution)/shard_map/psum | solution.py:143
  641.4 10.1 %fusion.46 = (bf16[1,128,16,256]{3,0,1,2:T(2,128)(2,1)S(1)}, bf16[1,128,16,256]{3,0,1,2:T(2,128)(2,1)S(1)}, bf16[1,128,16,256]{3,0,1,2:T(2,128)(2,1)S(1)}) fusion(bf16[3,128,16,256]{3,0,1,2:T(4,128)(2,1)} %bitcast.23), kind=kLoop, calls=%fused_computation.104 | loop fusion | bytes 6291456 | tf_op jit(solution)/shard_map/slice | solution.py:147
  659.1 1.7 broadcast_multiply_fusion
  (104 shorter events, 25.8 us)
Async XLA Ops:
  7.2 23.0 %copy-start = (f32[128,16]{0,1:T(8,128)S(1)}, f32[128,16]{0,1:T(8,128)}, u32[]{:S(2)}) copy-start(f32[128,16]{0,1:T(8,128)} %param.14) | copy-start | bytes 24580
  7.2 128.6 %all-gather.5.cloned.1.call-start = ((), (), s32[]{:S(2)}) async-start(), calls=%async_computation.4 | async-start | bytes 2228224 | tf_op jit(solution)/shard_map/all_gather | solution.py:115
  7.9 307.2 %all-gather.3.cloned.1.call-start = ((), (), s32[]{:S(2)}) async-start(), calls=%async_computation.3 | async-start | bytes 17825792 | tf_op jit(solution)/shard_map/all_gather | solution.py:100
  15.6 11.7 %copy-start.23 = (f32[3,7,256]{2,1,0:T(8,128)S(1)}, f32[3,7,256]{2,1,0:T(8,128)}, u32[]{:S(2)}) copy-start(f32[3,7,256]{2,1,0:T(8,128)} %param.13) | copy-start | bytes 64516
  15.6 102.9 %all-to-all-start = ((bf16[3,128,4096]{1,0,2:T(4,128)(2,1)}), bf16[3,128,4096]{1,0,2:T(4,128)(2,1)}, u32[]{:S(2)}, u32[]{:S(2)}) async-start(bf16[3,128,4096]{1,0,2:T(4,128)(2,1)} %copy.83), calls=%async_computation | async-start | bytes 8388608 | tf_op jit(solution)/shard_map/all_to_all | solution.py:116
  27.3 631.8 %reduce-scatter.2.cloned.1.call-start = ((), (), s32[]{:S(2)}) async-start(), calls=%async_computation.5 | async-start | bytes 4456448 | tf_op jit(solution)/shard_map/reduce_scatter | solution.py:107
  124.0 2.5 copy-start.10
  124.0 2.7 collective-permute-start
  126.5 2.7 copy-start.8
  315.1 19.4 %copy-start.9 = (f32[3,2048,256]{2,1,0:T(8,128)S(1)}, f32[3,2048,256]{2,1,0:T(8,128)}, u32[]{:S(2)}) copy-start(f32[3,2048,256]{2,1,0:T(8,128)} %multiply_add_fusion) | copy-start | bytes 18874372
  331.1 11.2 %copy-start.11 = (f32[2048,256]{1,0:T(8,128)}, f32[2048,256]{1,0:T(8,128)S(1)}, u32[]{:S(2)}) copy-start(f32[2048,256]{1,0:T(8,128)S(1)} %get-tuple-element.38) | copy-start | bytes 6291460
  331.1 21.1 %collective-permute-start.1 = (bf16[128,256]{1,0:T(8,128)(2,1)S(1)}, bf16[128,256]{1,0:T(8,128)(2,1)S(1)}, u32[]{:S(2)}, u32[]{:S(2)}) collective-permute-start(bf16[128,256]{1,0:T(8,128)(2,1)S(1)} %slice.279), channel_id=1, source_target_pairs={{0,16},{16,32},{32,48},{48,64},{64,80},{80,96},{96,112},{112,128},... | collective-permute-start | bytes 196616 | tf_op jit(solution)/shard_map/ppermute | solution.py:16
  343.7 3.0 copy-start.13
  346.7 2.3 copy-start.18
  346.7 5.5 copy-start.19
  350.7 16.3 %collective-permute-start.2 = (bf16[128,256]{1,0:T(8,128)(2,1)S(1)}, bf16[128,256]{1,0:T(8,128)(2,1)S(1)}, u32[]{:S(2)}, u32[]{:S(2)}) collective-permute-start(bf16[128,256]{1,0:T(8,128)(2,1)S(1)} %slice.278), channel_id=1, source_target_pairs={{16,0},{32,16},{48,32},{64,48},{80,64},{96,80},{112,96},{128,112},... | collective-permute-start | bytes 196616 | tf_op jit(solution)/shard_map/ppermute | solution.py:16
  352.3 4.0 copy-start.20
  354.1 5.0 copy-start.16
  354.1 5.0 copy-start.21
  356.3 2.9 copy-start.17
  373.1 5.0 copy-start.14
  373.1 5.0 copy-start.22
  381.7 5.1 copy-start.24
  392.8 1.3 copy-start.2
  392.8 2.1 copy-start.4
  392.8 2.8 copy-start.6
  392.8 4.5 copy-start.12
  395.6 15.1 %collective-permute-start.3 = (f32[3,6,256]{2,1,0:T(8,128)S(1)}, f32[3,6,256]{2,1,0:T(8,128)S(1)}, u32[]{:S(2)}, u32[]{:S(2)}) collective-permute-start(f32[3,6,256]{2,1,0:T(8,128)S(1)} %slice.164), channel_id=1, source_target_pairs={{16,0},{32,16},{48,32},{64,48},{80,64},{96,80},{112,96},{128,112},... | collective-permute-start | bytes 55304 | tf_op jit(solution)/shard_map/ppermute | solution.py:16
  428.5 6.6 copy-start.15
  428.5 212.9 %all-to-all-start.1 = ((bf16[3,2048,256]{2,0,1:T(4,128)(2,1)}), bf16[3,2048,256]{2,0,1:T(4,128)(2,1)}, u32[]{:S(2)}, u32[]{:S(2)}) async-start(bf16[3,2048,256]{2,0,1:T(4,128)(2,1)} %copy.103), calls=%async_computation.1 | async-start | bytes 8388608 | tf_op jit(solution)/shard_map/all_to_all | solution.py:140
  444.3 8.6 %copy-start.3 = (f32[2048,256]{1,0:T(8,128)S(1)}, f32[2048,256]{1,0:T(8,128)}, u32[]{:S(2)}) copy-start(f32[2048,256]{1,0:T(8,128)} %copy-done.2) | copy-start | bytes 6291460
  452.9 3.8 copy-start.5
  452.9 4.5 copy-start.7
  654.0 6.7 %copy-start.1 = (f32[128,16]{0,1:T(8,128)S(1)}, f32[128,16]{0,1:T(8,128)}, u32[]{:S(2)}) copy-start(f32[128,16]{0,1:T(8,128)} %param.14) | copy-start | bytes 24580
Sparse Core Ops, SparseCore 0:
  9.7 103.2 all-gather.4
  115.7 199.2 all-gather.2
  410.8 107.3 reduce-scatter.1
where the time goes:
time: 676 us; the launch traced here: 668 us
  waiting for transfers between devices  255 us (38%)
  blocking collectives  163 us (24%)
  local copies, waits for them, and re-layouts  77.6 us (11%)
  matrix products  71.3 us (11%)
  other arithmetic  59.4 us (9%)
  starting transfers between devices  26.6 us (4%)
  between operations  14.6 us (2%)
    all_gather x1, waiting for transfers between devices, cotangent_terms(): all_rows = lax.all_gather(cotangent, 'seq', axis=0, tiled=True)  179 us
    psum x1, blocking collectives, body(): lax.psum((short_part, long_part, gain_part), 'fsdp')  163 us
    all_to_all x1, waiting for transfers between devices, body(): lax.all_to_all(stacked, 'seq', split_axis=2, concat_axis=1, tiled=True)  74 us
    unnamed x70, local copies, waits for them, and re-layouts  25 us
    reduce_sum x2, other arithmetic, short_backward(): jnp.sum(feat_grad * extended[:, begin:begin + row_count], axis=1)  19.4 us
    dot_general x1, matrix products, cotangent_terms(): lax.dot_general(all_rows, full_cols, (((1,), (1,)), ((), ())), preferred_...  16 us
  transfers between devices with their start and end apart: 9, of which 3 were waited for; matrix products, arithmetic and copies ran while one was open for 24% of the time, Pallas kernels for 0%

commit v1 on v0

v1 whole, which is shorter than its diff:
```python
import functools
import jax
import jax.numpy as jnp
from jax import lax
from jax.experimental import pallas as pl
from jax.experimental.pallas import tpu as pltpu
from jax.sharding import Mesh, PartitionSpec as P

MESH = pl.DeviceIdType.MESH
HALO = 144
SHORT = 7
SCALE = 32768.0 ** -0.5
AXES = ("zl", "y", "zh", "x", "core")


def place():
    return tuple(lax.axis_index(a) for a in AXES)


def group_peer(offset):
    _, _, _, x, c = place()
    s = lax.rem(2 * x + c + offset, 8)
    return {"x": s // 2, "core": lax.rem(s, 2)}


def z_peer(offset):
    zl, _, zh, _, _ = place()
    p = lax.rem(4 * zh + zl + offset, 8)
    return {"zl": lax.rem(p, 4), "zh": p // 4}


def y_peer(offset):
    return {"y": lax.rem(lax.axis_index("y") + offset, 4)}


def x_peer(offset):
    return {"x": lax.rem(lax.axis_index("x") + offset, 4)}


def block_peer(offset):
    zl, y, zh, _, _ = place()
    n = lax.rem(8 * zl + 2 * y + zh + offset, 32)
    return {"zl": n // 8, "y": lax.rem(n // 2, 4), "zh": lax.rem(n, 2)}


def greet(peers):
    barrier = pltpu.get_barrier_semaphore()
    for peer in peers:
        pl.semaphore_signal(barrier, inc=1, device_id=peer, device_id_type=MESH)
    pl.semaphore_wait(barrier, len(peers))


def remote(src, dst, send_sem, recv_sem, peer):
    return pltpu.make_async_remote_copy(
        src_ref=src, dst_ref=dst, send_sem=send_sem, recv_sem=recv_sem, device_id=peer, device_id_type=MESH
    )


def landed(ref, sem):
    pltpu.make_async_copy(ref, ref, sem).wait()


def gather_kernel(q, k, v, cot, w, short, tabs, gain, ext, cotg, wg, shorts, tabss, gains, a2a_s, a2a_r, halo_s, halo_r, cot_s, cot_r, wz_s, wz_r, wy_s, wy_r, own, sm_s, sm_r):
    zl, y, zh, x, c = place()
    s = 2 * x + c
    f = 4 * zl + y
    greet(
        [group_peer(o) for o in range(1, 8)]
        + [z_peer(o) for o in range(1, 8)]
        + [y_peer(o) for o in range(1, 4)]
        + [block_peer(1), block_peer(31)]
    )
    pending = []

    def rows_of(src):
        return pl.ds(pl.multiple_of(HALO + 128 * src, 16), 128)

    def cot_rows(src):
        return pl.ds(pl.multiple_of(128 * src, 128), 128)

    def w_block(zh_, f_):
        return wg.at[pl.ds(pl.multiple_of(256 * zh_, 256), 256), pl.ds(pl.multiple_of(256 * f_, 256), 256)]

    small = ((short, shorts), (tabs, tabss), (gain, gains))
    own_small = [pltpu.make_async_copy(src, dst.at[zh], own.at[2 + i]) for i, (src, dst) in enumerate(small)]
    for i, (src, dst) in enumerate(small):
        cp = remote(src, dst.at[zh], sm_s.at[i], sm_r.at[i], z_peer(4))
        cp.start()
        own_small[i].start()
        pending.append(cp)
    own_w = pltpu.make_async_copy(w, w_block(zh, f), own.at[0])
    own_w.start()
    for o in range(1, 8):
        cp = remote(w, w_block(zh, f), wz_s.at[o], wz_r.at[o], z_peer(o))
        cp.start()
        pending.append(cp)
    for o in (2, 6, 3, 5, 4, 7, 1, 0):
        d = lax.rem(s + o, 8)
        for slab in range(2):
            cols = pl.ds(pl.multiple_of(2048 * slab + 256 * d, 256), 256)
            for i, src in enumerate((q, k, v)):
                if o:
                    cp = remote(src.at[:, cols], ext.at[i, slab, rows_of(s), :], a2a_s.at[o], a2a_r.at[o], group_peer(o))
                    cp.start()
                else:
                    cp = pltpu.make_async_copy(src.at[:, cols], ext.at[i, slab, rows_of(s), :], a2a_s.at[0])
                    cp.start()
    sib = {"core": 1 - c}
    own_c = pltpu.make_async_copy(cot, cotg.at[cot_rows(s), :], own.at[1])
    own_c.start()
    right = remote(cot, cotg.at[cot_rows(s), :], cot_s.at[0], cot_r.at[0], x_peer(1))
    left = remote(cot, cotg.at[cot_rows(s), :], cot_s.at[1], cot_r.at[1], x_peer(3))
    over = remote(cot, cotg.at[cot_rows(s), :], cot_s.at[2], cot_r.at[2], sib)
    right.start()
    left.start()
    over.start()
    pending += [right, left, over]
    own_w.wait()
    for o in range(1, 8):
        landed(w_block(0, 0), wz_r.at[o])
    ycols = lambda zl_, y_: wg.at[:, pl.ds(pl.multiple_of(1024 * zl_ + 256 * y_, 256), 256)]
    for zl_ in range(4):
        for way, off in ((0, 1), (1, 3)):
            cp = remote(ycols(zl_, y), ycols(zl_, y), wy_s.at[way, zl_], wy_r.at[way, zl_], y_peer(off))
            cp.start()
            pending.append(cp)
    s_left = lax.rem(s + 6, 8)
    s_right = lax.rem(s + 2, 8)
    s_far = lax.rem(s + 4, 8)
    lo = lambda src: cotg.at[pl.ds(pl.multiple_of(128 * src, 128), 64), :]
    hi = lambda src: cotg.at[pl.ds(pl.multiple_of(128 * src + 64, 64), 64), :]
    landed(cot, cot_r.at[0])
    steps = [
        remote(lo(s_left), lo(s_left), cot_s.at[3], cot_r.at[3], x_peer(1)),
        remote(cotg.at[cot_rows(s_left), :], cotg.at[cot_rows(s_left), :], cot_s.at[4], cot_r.at[4], sib),
    ]
    for cp in steps:
        cp.start()
    pending += steps
    landed(cot, cot_r.at[1])
    steps = [
        remote(hi(s_right), hi(s_right), cot_s.at[5], cot_r.at[5], x_peer(3)),
        remote(cotg.at[cot_rows(s_right), :], cotg.at[cot_rows(s_right), :], cot_s.at[6], cot_r.at[6], sib),
    ]
    for cp in steps:
        cp.start()
    pending += steps
    y_left, y_right = lax.rem(y + 3, 4), lax.rem(y + 1, 4)
    for zl_ in range(4):
        landed(ycols(0, 0), wy_r.at[0, zl_])
        if zl_ < 2:
            cp = remote(ycols(zl_, y_left), ycols(zl_, y_left), wy_s.at[2, zl_], wy_r.at[2, zl_], y_peer(1))
            cp.start()
            pending.append(cp)
    for zl_ in range(4):
        landed(ycols(0, 0), wy_r.at[1, zl_])
        if zl_ >= 2:
            cp = remote(ycols(zl_, y_right), ycols(zl_, y_right), wy_s.at[2, zl_], wy_r.at[2, zl_], y_peer(3))
            cp.start()
            pending.append(cp)
    for o in range(8):
        src = lax.rem(s + 8 - o, 8)
        landed(ext.at[:, :, rows_of(src), :], a2a_r.at[o] if o else a2a_s.at[0])
    last = [
        remote(ext.at[1:3, :, 1024:1168, :], ext.at[1:3, :, 0:144, :], halo_s.at[0], halo_r.at[0], block_peer(1)),
        remote(ext.at[0, :, 1152:1168, :], ext.at[0, :, 128:144, :], halo_s.at[1], halo_r.at[1], block_peer(1)),
    ]
    for cp in last:
        cp.start()
    own_c.wait()
    landed(lo(0), cot_r.at[3])
    cp = remote(lo(s_far), lo(s_far), cot_s.at[7], cot_r.at[7], sib)
    cp.start()
    pending.append(cp)
    landed(lo(0), cot_r.at[5])
    cp = remote(hi(s_far), hi(s_far), cot_s.at[8], cot_r.at[8], sib)
    cp.start()
    pending.append(cp)
    landed(cot, cot_r.at[2])
    landed(cot, cot_r.at[4])
    landed(cot, cot_r.at[6])
    landed(lo(0), cot_r.at[7])
    landed(lo(0), cot_r.at[8])
    for zl_ in range(4):
        landed(ycols(0, 0), wy_r.at[2, zl_])
    for cp in last:
        cp.wait()
    for o in range(1, 8):
        landed(ext.at[:, :, rows_of(0), :], a2a_s.at[o])
    for cp in pending:
        cp.wait_send()
    for i, (src, dst) in enumerate(small):
        own_small[i].wait()
        landed(src, sm_r.at[i])


ANY = pl.BlockSpec(memory_space=pl.ANY)


def gather(q, k, v, cot, w, short, tabs, gain):
    dma = pltpu.SemaphoreType.DMA
    f32 = lambda *shape: jax.ShapeDtypeStruct(shape, jnp.float32)
    return pl.pallas_call(
        gather_kernel,
        out_shape=(
            jax.ShapeDtypeStruct((3, 2, 1024 + HALO, 256), jnp.bfloat16),
            jax.ShapeDtypeStruct((1024, 4096), jnp.bfloat16),
            jax.ShapeDtypeStruct((512, 4096), jnp.bfloat16),
            f32(2, 3, SHORT, 256),
            f32(2, 2, 16, 256),
            f32(2, 1, 256),
        ),
        in_specs=[ANY] * 8,
        out_specs=(ANY,) * 6,
        scratch_shapes=[dma((8,)), dma((8,)), dma((2,)), dma((2,)), dma((9,)), dma((9,)), dma((8,)), dma((8,)), dma((3, 4)), dma((3, 4)), dma((5,)), dma((3,)), dma((3,))],
        compiler_params=pltpu.CompilerParams(collective_id=0, has_side_effects=True),
        name="gather_inputs",
    )(q, k, v, cot, w, short, tabs, gain)


def spread(tiles, lane):
    tiles = list(tiles)
    for k in (1, 2, 4):
        keep = (lane // (16 * k)) % 2 == 0
        for i in range(8):
            if not i & k:
                a, b = tiles[i], tiles[i + k]
                tiles[i] = jnp.where(keep, a, pltpu.roll(b, 16 * k, 1))
                tiles[i + k] = jnp.where(keep, pltpu.roll(a, 128 - 16 * k, 1), b)
    return tiles


def forward_kernel(ext, mg, taps, revs, gain, f1_o, f2_o, p_o, qf_o, sl_o, mix_o, pg_o, dg_o, stage, prod, group):
    zl, y, zh, _, _ = place()
    started = 8 * zl + 2 * y + zh > 0
    for i in range(3):
        lead = ext[i, 0, 0:HALO, :].astype(jnp.float32)
        stage[i, 0:HALO, :] = jnp.where(started, lead, 0.0)
    mass = 128

    @pl.loop(0, 8)
    def _(b):
        r = pl.multiple_of(HALO + mass * b, 16)
        for i in range(3):
            stage[i, pl.ds(r, mass), :] = ext[i, 0, pl.ds(r, mass), :].astype(jnp.float32)

    def feature(i, r, rows):
        total = taps[0, i, 0:1, :] * stage[i, pl.ds(r, rows), :]
        for j in range(1, SHORT):
            total = total + taps[0, i, j : j + 1, :] * stage[i, pl.ds(r - j, rows), :]
        return total

    @pl.loop(0, 2)
    def _(b):
        r = HALO - 128 + 64 * b
        prod[pl.ds(pl.multiple_of(64 * b, 64), 64), :] = feature(1, r, 64) * feature(2, r, 64)

    @pl.loop(0, 16)
    def _(b):
        r = HALO + 64 * b
        here = pl.multiple_of(64 * b, 64)
        one, two = feature(1, r, 64), feature(2, r, 64)
        f1_o[pl.ds(here, 64), :] = one.astype(jnp.bfloat16)
        f2_o[pl.ds(here, 64), :] = two.astype(jnp.bfloat16)
        both = one * two
        prod[pl.ds(here + 128, 64), :] = both
        p_o[pl.ds(here, 64), :] = both.astype(jnp.bfloat16)

    lane = lax.broadcasted_iota(jnp.int32, (16, 128), 1)

    @pl.loop(0, 8)
    def _(m):
        r = pl.multiple_of(16 * m, 16)
        now = spread([prod[pl.ds(128 + 128 * b + r, 16), :] for b in range(8)], lane)
        lead = prod[pl.ds(r, 16), :]
        for g in range(8):
            head = lead if g == 0 else pltpu.roll(lead, 128 - 16 * g, 1)
            before = jnp.where(lane < 16, head, pltpu.roll(now[g], 16, 1))
            pg_o[g, pl.ds(r, 16), :] = before.astype(jnp.bfloat16)
            pg_o[g, pl.ds(128 + r, 16), :] = now[g].astype(jnp.bfloat16)

    for g in range(8):
        table = pltpu.roll(jnp.broadcast_to(revs[0, 0, g : g + 1, :], (128, 256)), 0, 1, stride=1, stride_axis=0)
        group[g] = jnp.dot(table.astype(jnp.bfloat16), pg_o[g], preferred_element_type=jnp.float32)

    @pl.loop(0, 8)
    def _(m):
        r = pl.multiple_of(16 * m, 16)
        filt = spread([group[g, pl.ds(r, 16), :] for g in range(8)], lane)
        slopes = []
        for b in range(8):
            here = pl.ds(pl.multiple_of(128 * b + r, 16), 16)
            whole = filt[b] + gain[0] * prod[pl.ds(128 * (b + 1) + r, 16), :]
            lead = feature(0, HALO + 128 * b + r, 16)
            back = mg[here, :]
            mix_o[here, :] = (lead * whole).astype(jnp.bfloat16)
            qf_o[here, :] = (back * whole).astype(jnp.bfloat16)
            slope = back * lead
            sl_o[here, :] = slope.astype(jnp.bfloat16)
            slopes.append(slope)
        slopes = spread(slopes, lane)
        for g in range(8):
            dg_o[g, pl.ds(r, 16), :] = slopes[g].astype(jnp.bfloat16)


def forward(ext, mg, taps, revs, gain):
    bf = lambda *shape: jax.ShapeDtypeStruct(shape, jnp.bfloat16)
    nat = pl.BlockSpec((1024, 128), lambda p: (0, p))
    return pl.pallas_call(
        forward_kernel,
        grid=(4,),
        out_shape=(bf(1024, 512),) * 6 + (bf(32, 256, 128), bf(32, 128, 128)),
        in_specs=[
            pl.BlockSpec((3, 1, 1024 + HALO, 128), lambda p: (0, p // 2, 0, p % 2)),
            nat,
            pl.BlockSpec((1, 3, SHORT, 128), lambda p: (p // 2, 0, 0, p % 2)),
            pl.BlockSpec((1, 1, 8, 256), lambda p: (p // 2, 0, p % 2, 0)),
            pl.BlockSpec((1, 1, 128), lambda p: (p // 2, 0, p % 2)),
        ],
        out_specs=(nat,) * 6 + (pl.BlockSpec((8, 256, 128), lambda p: (p, 0, 0)), pl.BlockSpec((8, 128, 128), lambda p: (p, 0, 0))),
        scratch_shapes=[
            pltpu.VMEM((3, 1024 + HALO, 128), jnp.float32),
            pltpu.VMEM((1152, 128), jnp.float32),
            pltpu.VMEM((8, 128, 128), jnp.float32),
        ],
        compiler_params=pltpu.CompilerParams(vmem_limit_bytes=40 * 2**20),
        name="mixer_forward",
    )(ext, mg, taps, revs, gain)


def weight_kernel(mix, cot, out, turned):
    @pl.when(pl.program_id(0) == 0)
    def _():
        for k in range(4):
            turned[pl.ds(128 * k, 128), :] = mix[:, pl.ds(128 * k, 128)].T

    part = jnp.dot(turned[...], cot[...], preferred_element_type=jnp.float32).astype(jnp.bfloat16)
    out[0, 0, 0] = part[:256]
    out[0, 0, 1] = part[256:]


def weight_part(mix, cot):
    return pl.pallas_call(
        weight_kernel,
        grid=(16,),
        out_shape=jax.ShapeDtypeStruct((4, 4, 2, 256, 256), jnp.bfloat16),
        in_specs=[pl.BlockSpec((1024, 512), lambda f: (0, 0)), pl.BlockSpec((1024, 256), lambda f: (0, f))],
        out_specs=pl.BlockSpec((1, 1, 2, 256, 256), lambda f: (f % 4, f // 4, 0, 0, 0)),
        scratch_shapes=[pltpu.VMEM((512, 1024), jnp.bfloat16)],
        compiler_params=pltpu.CompilerParams(vmem_limit_bytes=40 * 2**20),
        cost_estimate=pl.CostEstimate(flops=2 * 512 * 4096 * 1024, bytes_accessed=14 * 2**20, transcendentals=0),
        name="weight_part",
    )(mix, cot)


def backward_kernel(ext, dg, pg, sl, p, f1, f2, qf, edge, taps, fwds, gain, grad_o, short_o, long_o, stage, feat, group):
    zl, y, zh, _, _ = place()
    started = 8 * zl + 2 * y + zh > 0
    for i in range(3):
        lead = ext[i, 0, HALO - 16 : HALO, :].astype(jnp.float32)
        stage[i, 0:16, :] = jnp.where(started, lead, 0.0)

    @pl.loop(0, 8)
    def _(b):
        for i in range(3):
            stage[i, pl.ds(pl.multiple_of(16 + 128 * b, 16), 128), :] = ext[i, 0, pl.ds(pl.multiple_of(HALO + 128 * b, 16), 128), :].astype(jnp.float32)

    wide = lax.broadcasted_iota(jnp.int32, (128, 128), 1)
    lane = lax.broadcasted_iota(jnp.int32, (16, 128), 1)
    after = edge[0:128, :].astype(jnp.float32)
    tail = jnp.concatenate([edge[0:HALO, :], jnp.zeros((256 - HALO, 128), jnp.bfloat16)], 0)
    over = jnp.zeros((16, 128), jnp.float32)
    square = [lax.broadcasted_iota(jnp.int32, (256, 256), a) for a in (0, 1)]
    flip = (square[0] + square[1] == 255).astype(jnp.bfloat16)
    for g in range(8):
        table = pltpu.roll(jnp.broadcast_to(fwds[0, 0, g : g + 1, :], (128, 256)), 0, 1, stride=1, stride_axis=0).astype(jnp.bfloat16)
        here = dg[g]
        head = after if g == 7 else pltpu.roll(after, 16 * (7 - g), 1)
        later = jnp.where(wide >= 112, head, pltpu.roll(here.astype(jnp.float32), 112, 1)).astype(jnp.bfloat16)
        group[g] = jnp.dot(table[:, :128], here, preferred_element_type=jnp.float32) + jnp.dot(table[:, 128:], later, preferred_element_type=jnp.float32)
        past = jnp.dot(table[:16], tail, preferred_element_type=jnp.float32)
        over = jnp.where(lane // 16 == g, past, over)
        back = jnp.dot(flip, pg[g], preferred_element_type=jnp.float32).astype(jnp.bfloat16)
        gram = lax.dot_general(here, back, (((1,), (1,)), ((), ())), preferred_element_type=jnp.float32)
        lined = pltpu.roll(gram, 0, 1, stride=1, stride_axis=0)
        long_o[g : g + 1, :] = jnp.sum(lined, axis=0, keepdims=True)

    def gain_sum(m, total):
        r = pl.multiple_of(16 * m, 16)
        back = spread([group[g, pl.ds(r, 16), :] for g in range(8)], lane)
        for b in range(8):
            here = pl.ds(pl.multiple_of(128 * b + r, 16), 16)
            slope = sl[here, :].astype(jnp.float32)
            whole = back[b] + gain[0] * slope
            feat[0, here, :] = qf[here, :].astype(jnp.float32)
            feat[1, here, :] = whole * f2[here, :].astype(jnp.float32)
            feat[2, here, :] = whole * f1[here, :].astype(jnp.float32)
            term = slope * p[here, :].astype(jnp.float32)
            total = total + term[:8] + term[8:]
        return total

    total = lax.fori_loop(0, 8, gain_sum, jnp.zeros((8, 128), jnp.float32))
    over = over + gain[0] * edge[0:16, :].astype(jnp.float32)
    feat[0, 1024:1040, :] = edge[HALO + 32 : HALO + 48, :].astype(jnp.float32)
    feat[1, 1024:1040, :] = over * edge[HALO + 16 : HALO + 32, :].astype(jnp.float32)
    feat[2, 1024:1040, :] = over * edge[HALO : HALO + 16, :].astype(jnp.float32)

    for i in range(3):

        def rows_sum(b, sums):
            r = 64 * b
            grad = taps[0, i, 0:1, :] * feat[i, pl.ds(r, 64), :]
            for j in range(1, SHORT):
                grad = grad + taps[0, i, j : j + 1, :] * feat[i, pl.ds(r + j, 64), :]
            grad_o[i, 0, pl.ds(pl.multiple_of(r, 64), 64), :] = grad.astype(jnp.bfloat16)
            mine = feat[i, pl.ds(r, 64), :]
            out = []
            for j in range(SHORT):
                term = mine * stage[i, pl.ds(16 + r - j, 64), :]
                out.append(sums[j] + jnp.sum(term.reshape(8, 8, 128), axis=0))
            return tuple(out)

        sums = lax.fori_loop(0, 16, rows_sum, (jnp.zeros((8, 128), jnp.float32),) * SHORT)
        for j in range(SHORT):
            short_o[8 * i + j : 8 * i + j + 1, :] = jnp.sum(sums[j], axis=0, keepdims=True)
        short_o[8 * i + SHORT : 8 * i + 8, :] = jnp.sum(total, axis=0, keepdims=True)


def backward(ext, dg, pg, sl, p, f1, f2, qf, edge, taps, fwds, gain):
    nat = pl.BlockSpec((1024, 128), lambda q: (0, q))
    return pl.pallas_call(
        backward_kernel,
        grid=(4,),
        out_shape=(
            jax.ShapeDtypeStruct((3, 2, 1024, 256), jnp.bfloat16),
            jax.ShapeDtypeStruct((24, 512), jnp.float32),
            jax.ShapeDtypeStruct((32, 256), jnp.float32),
        ),
        in_specs=[
            pl.BlockSpec((3, 1, 1024 + HALO, 128), lambda q: (0, q // 2, 0, q % 2)),
            pl.BlockSpec((8, 128, 128), lambda q: (q, 0, 0)),
            pl.BlockSpec((8, 256, 128), lambda q: (q, 0, 0)),
        ]
        + [nat] * 5
        + [
            pl.BlockSpec((HALO + 48, 128), lambda q: (0, q)),
            pl.BlockSpec((1, 3, SHORT, 128), lambda q: (q // 2, 0, 0, q % 2)),
            pl.BlockSpec((1, 1, 8, 256), lambda q: (q // 2, 1, q % 2, 0)),
            pl.BlockSpec((1, 1, 128), lambda q: (q // 2, 0, q % 2)),
        ],
        out_specs=(
            pl.BlockSpec((3, 1, 1024, 128), lambda q: (0, q // 2, 0, q % 2)),
            pl.BlockSpec((24, 128), lambda q: (0, q)),
            pl.BlockSpec((8, 256), lambda q: (q, 0)),
        ),
        scratch_shapes=[
            pltpu.VMEM((3, 1024 + 16, 128), jnp.float32),
            pltpu.VMEM((3, 1024 + 16, 128), jnp.float32),
            pltpu.VMEM((8, 128, 128), jnp.float32),
        ],
        compiler_params=pltpu.CompilerParams(vmem_limit_bytes=40 * 2**20),
        name="mixer_backward",
    )(ext, dg, pg, sl, p, f1, f2, qf, edge, taps, fwds, gain)


def return_kernel(grad, part, gq, gk, gv, wout, mine, land, once, zland, a2a_s, a2a_r, own, wy_s, wy_r, wz_s, wz_r):
    zl, y, zh, x, c = place()
    s = 2 * x + c
    zpos = 4 * zh + zl
    greet([group_peer(o) for o in range(1, 8)] + [z_peer(o) for o in range(1, 8)] + [y_peer(o) for o in range(1, 4)])
    order = (4, 3, 5, 2, 6, 1, 7, 0)

    fetch = pltpu.make_async_copy(part.at[y], mine, own)
    fetch.start()
    to_y = []
    for k in order:
        t = lax.rem(zpos + k, 8)
        for o in range(1, 4):
            cp = remote(
                part.at[lax.rem(y + o, 4), lax.rem(t, 4), t // 4], land.at[o - 1, k], wy_s.at[o - 1, k], wy_r.at[o - 1, k], y_peer(o)
            )
            cp.start()
            to_y.append(cp)
    for o in (2, 6, 3, 5, 4, 7, 1, 0):
        d = lax.rem(s + o, 8)
        for slab in range(2):
            cols = pl.ds(pl.multiple_of(2048 * slab + 256 * s, 256), 256)
            for i, dst in enumerate((gq, gk, gv)):
                src = grad.at[i, slab, pl.ds(pl.multiple_of(128 * d, 128), 128), :]
                if o:
                    remote(src, dst.at[:, cols], a2a_s.at[o], a2a_r.at[o], group_peer(o)).start()
                else:
                    pltpu.make_async_copy(src, dst.at[:, cols], a2a_s.at[0]).start()
    fetch.wait()
    to_z = []
    for k in order:
        t = lax.rem(zpos + k, 8)
        for o in range(3):
            landed(land.at[o, k], wy_r.at[o, k])

        @pl.loop(0, 4)
        def _(n):
            rows = pl.ds(pl.multiple_of(64 * n, 64), 64)
            total = mine[lax.rem(t, 4), t // 4, rows, :].astype(jnp.float32)
            for o in range(3):
                total = total + land[o, k, rows, :].astype(jnp.float32)
            once[k, rows, :] = total.astype(jnp.bfloat16)

        if k:
            cp = remote(once.at[k], zland.at[k], wz_s.at[k], wz_r.at[k], z_peer(k))
            cp.start()
            to_z.append(cp)
    for k in range(1, 8):
        landed(zland.at[k], wz_r.at[k])

    @pl.loop(0, 4)
    def _(n):
        rows = pl.ds(pl.multiple_of(64 * n, 64), 64)
        total = once[0, rows, :].astype(jnp.float32)
        for k in range(1, 8):
            total = total + zland[k, rows, :].astype(jnp.float32)
        wout[rows, :] = total * SCALE

    for cp in to_y + to_z:
        cp.wait_send()
    six = grad.at[:, :, 0:128, :]
    for o in range(8):
        landed(six, a2a_s.at[o])
        if o:
            landed(six, a2a_r.at[o])


def give_back(grad, part):
    dma = pltpu.SemaphoreType.DMA
    tok = jax.ShapeDtypeStruct((128, 4096), jnp.bfloat16)
    return pl.pallas_call(
        return_kernel,
        out_shape=(tok, tok, tok, jax.ShapeDtypeStruct((256, 256), jnp.float32)),
        in_specs=[ANY] * 2,
        out_specs=(ANY,) * 3 + (pl.BlockSpec(memory_space=pltpu.VMEM),),
        scratch_shapes=[
            pltpu.VMEM((4, 2, 256, 256), jnp.bfloat16),
            pltpu.VMEM((3, 8, 256, 256), jnp.bfloat16),
            pltpu.VMEM((8, 256, 256), jnp.bfloat16),
            pltpu.VMEM((8, 256, 256), jnp.bfloat16),
            dma((8,)),
            dma((8,)),
            dma,
            dma((3, 8)),
            dma((3, 8)),
            dma((8,)),
            dma((8,)),
        ],
        compiler_params=pltpu.CompilerParams(collective_id=1, has_side_effects=True, vmem_limit_bytes=40 * 2**20),
        name="return_grads",
    )(grad, part)


def body(q, k, v, cot, w, short_taps, long_taps, skip_gain):
    blank = jnp.zeros((16, 1), jnp.float32)
    turned = long_taps.T
    tables = jnp.stack(
        [
            jnp.concatenate([blank, turned[:, ::-1], jnp.zeros((16, 127), jnp.float32)], 1),
            jnp.concatenate([turned, jnp.zeros((16, 128), jnp.float32)], 1),
        ]
    )
    ext, cotg, wg, taps, tables, gain = gather(q, k, v, cot, w, short_taps, tables, skip_gain[None, :])
    mg = lax.dot_general(cotg, wg, (((1,), (1,)), ((), ())), preferred_element_type=jnp.float32)
    f1, f2, p, qf, sl, mix, pg, dg = forward(ext, mg, taps, tables, gain)
    edge = jnp.concatenate([sl[:HALO], f1[:16], f2[:16], qf[:16]], 0)
    route = [(i + 1, i) for i in range(31)]
    edge = lax.ppermute(edge, ("zl", "y", "zh"), route)
    part = weight_part(mix, cotg)
    grad, short, long = backward(ext, dg, pg, sl, p, f1, f2, qf, edge, taps, tables, gain)
    short, long = lax.psum((short, long), ("zl", "y", "zh"))
    gq, gk, gv, wout = give_back(grad, part)
    zh = lax.axis_index("zh")
    short = lax.dynamic_slice_in_dim(short, 256 * zh, 256, 1) * SCALE
    long = lax.dynamic_slice_in_dim(long, 16 * zh, 16, 0)[:, 127:255].T * SCALE
    return gq, gk, gv, wout, short.reshape(3, 8, 256)[:, :SHORT], long, short[SHORT]


def solution(mesh):
    fine = Mesh(mesh.devices.reshape(4, 4, 2, 4, 2), AXES)
    tok = P(AXES, None)
    chan = ("zh", "x", "core")
    weight = P(chan, ("zl", "y"))
    small = (P(None, None, chan), P(None, chan), P(chan))
    return jax.shard_map(
        body,
        mesh=fine,
        in_specs=(tok,) * 4 + (weight,) + small,
        out_specs=(tok,) * 3 + (weight,) + small,
        check_vma=False,
    )
```

time: 676 us -> 333 us (0.49); the launches traced: 668 us -> 332 us
  Pallas kernels: 0 us -> 196 us
  waiting for transfers between devices: 255 us -> 86.7 us
  blocking collectives: 163 us -> 0 us
  matrix products: 71.3 us -> 8.24 us
  local copies, waits for them, and re-layouts: 77.6 us -> 20.3 us
  other arithmetic: 59.4 us -> 4.89 us
  starting transfers between devices: 26.6 us -> 1.33 us
    pallas_call x0 -> x5, Pallas kernels: none -> 196 us  [the longest x1 87.7 us: gather(): pl.pallas_call(gather_kernel, out_shape=(jax.ShapeDtypeStruct((3, 2, 1024...]
    all_gather x2 -> x0, waiting for transfers between devices: 179 us -> none  [the longest x1 179 us: cotangent_terms(): all_rows = lax.all_gather(cotangent, 'seq', axis=0, tiled=True)]
    psum x1 -> x0, blocking collectives: 163 us -> none  [body(): lax.psum((short_part, long_part, gain_part), 'fsdp')]
    all_to_all x2 -> x0, waiting for transfers between devices: 74 us -> none  [the longest x1 74 us: body(): lax.all_to_all(stacked, 'seq', split_axis=2, concat_axis=1, tiled=True)]
    psum x0 -> x1, waiting for transfers between devices: none -> 69.4 us  [body(): short, long = lax.psum((short, long), ('zl', 'y', 'zh'))]
    dot_general x12 -> x1, matrix products: 71.3 us -> 8.24 us  [body(): lax.dot_general(cotg, wg, (((1,), (1,)), ((), ())), preferred_element_typ...]
    reduce_sum x2 -> x0, other arithmetic: 19.4 us -> none  [short_backward(): jnp.sum(feat_grad * extended[:, begin:begin + row_count], axis=1)]
    all_to_all x2 -> x0, starting transfers between devices: 18.2 us -> none  [the longest x1 11.6 us: body(): lax.all_to_all(stacked, 'seq', split_axis=2, concat_axis=1, tiled=True)]
  transfers between devices with their start and end apart: 9 -> 2, of which waited for: 3 -> 2; matrix products, arithmetic and copies ran while one was open for 24% -> 0% of each run, Pallas kernels for 0% -> 18%
where the time goes in v1:
time: 333 us; the launch traced here: 332 us
  Pallas kernels  196 us (59%)
  waiting for transfers between devices  86.7 us (26%)
  local copies, waits for them, and re-layouts  20.3 us (6%)
  between operations  14.2 us (4%)
  matrix products  8.24 us (2%)
  other arithmetic  4.89 us (1%)
    pallas_call x1, Pallas kernels, gather(): pl.pallas_call(gather_kernel, out_shape=(jax.ShapeDtypeStruct((3, 2, 1024...  87.7 us
    psum x1, waiting for transfers between devices, body(): short, long = lax.psum((short, long), ('zl', 'y', 'zh'))  69.4 us
    pallas_call x1, Pallas kernels, give_back(): pl.pallas_call(return_kernel, out_shape=(tok, tok, tok, jax.ShapeDtypeStr...  50.6 us
    pallas_call x1, Pallas kernels, forward(): pl.pallas_call(forward_kernel, grid=(4,), out_shape=(bf(1024, 512),) * 6...  25.4 us
    pallas_call x1, Pallas kernels, backward(): pl.pallas_call(backward_kernel, grid=(4,), out_shape=(jax.ShapeDtypeStruc...  23.8 us
    unnamed x28, local copies, waits for them, and re-layouts  18.9 us
    ppermute x1, waiting for transfers between devices, body(): edge = lax.ppermute(edge, ('zl', 'y', 'zh'), route)  17.3 us
    pallas_call x1, Pallas kernels, weight_part(): pl.pallas_call(weight_kernel, grid=(16,), out_shape=jax.ShapeDtypeStruct(...  8.74 us
  transfers between devices with their start and end apart: 2, of which 2 were waited for; matrix products, arithmetic and copies ran while one was open for 0% of the time, Pallas kernels for 18%

profile of v1, /device:TPU:2, one launch (start us, length us, event | category | flops | bytes accessed | tf_op | source)
XLA Modules:
  0.0 332.0 jit_solution(12656174963613360933)
XLA Ops:
  7.2 0.0 all-reduce.4.cloned.1.call-start
  7.2 0.8 rev.3
  8.0 0.1 pad.9.clone
  8.1 0.8 maximum_bitcast_fusion
  8.8 0.6 pad_maximum_fusion.1.tabs
  9.5 87.7 %gather_inputs.1 = (bf16[3,2,1168,256]{3,2,1,0:T(8,128)(2,1)}, bf16[1024,4096]{1,0:T(8,128)(2,1)}, bf16[512,4096]{1,0:T(8,128)(2,1)}, f32[2,3,7,256]{3,2,1,0:T(8...) custom-call(bf16[128,4096]{1,0:T(8,128)(2,1)} %q.1, bf16[128,4096]{1,0:T(8,128)(2,1)} %k.1, bf16[128,4096]{1,0:T(8,128)(2,1)} %v.1, ...), custom_call_target="tpu_custom_call" | custom-call | tf_op jit(solution)/shard_map/gather_inputs/pallas_call | solution.py:203
  97.2 0.0 copy-start.6
  97.2 0.0 copy-start.7
  97.2 0.0 copy-start.8
  97.2 8.2 %fusion.1.mg = f32[1024,512]{1,0:T(8,128)S(1)} fusion(bf16[1024,4096]{1,0:T(8,128)(2,1)} %get-tuple-element.29.cot, bf16[512,4096]{1,0:T(8,128)(2,1)} %get-tuple-element.30), kind=kOutput, calls=%fused_computation.7 | convolution fusion | flops 4294967296 | bytes 14680064 | tf_op jit(solution)/shard_map/dot_general | solution.py:569
  105.5 0.0 copy-done.6
  105.5 0.0 copy-done.7
  105.5 0.0 copy-done.8
  105.5 25.4 %mixer_forward.1 = (bf16[1024,512]{1,0:T(8,128)(2,1)S(1)}, bf16[1024,512]{1,0:T(8,128)(2,1)S(1)}, bf16[1024,512]{1,0:T(8,128)(2,1)S(1)}, bf16[1024,512]{1,0:T(8,...) custom-call(bf16[3,2,1168,256]{3,2,1,0:T(8,128)(2,1)} %get-tuple-ele, ...), custom_call_target="tpu_custom_call" | custom-call | tf_op jit(solution)/shard_map/mixer_forward/pallas_call | solution.py:309
  131.0 0.0 copy-start.10
  131.0 1.0 copy-done.10
  132.0 1.3 collective-permute-start
  133.3 17.3 %collective-permute-done.edge = bf16[192,512]{1,0:T(8,128)(2,1)S(1)} collective-permute-done((bf16[192,512]{1,0:T(8,128)(2,1)S(1)}, bf16[192,512]{1,0:T(8,128)(2,1)S(1)}, u32[]{:S(2)}, u32[]{:S(2)}) %collective-permute-start) | collective-permute-done | bytes 196640 | tf_op jit(solution)/shard_map/ppermute | solution.py:573
  150.6 23.8 %mixer_backward.1 = (bf16[3,2,1024,256]{3,2,1,0:T(8,128)(2,1)S(1)}, f32[24,512]{1,0:T(8,128)}, f32[32,256]{1,0:T(8,128)}) custom-call(bf16[3,2,1168,256]{3,2,1,0:T(8,128)(2,1)} %get-tuple-element.28.ext, bf16[32,128,128]{2,1,0:T(8,128)(2,1)S(1)} %get-tuple-element.34.dg, bf16[32,256,128]{2,1,0:T(8,128)(2,1)S(1)} %get-tuple-element.35.pg, ...), custom_call_target="tpu_custom_call" | custom-call | tf_op jit(solution)/shard_map/mixer_backward/pallas_call | solution.py:431
  174.4 0.0 all-reduce.4.cloned.1.call-update
  174.4 0.0 copy-start.9
  174.4 3.4 %copy-done.9 = bf16[1024,4096]{1,0:T(8,128)(2,1)S(1)} copy-done((bf16[1024,4096]{1,0:T(8,128)(2,1)S(1)}, bf16[1024,4096]{1,0:T(8,128)(2,1)}, u32[]{:S(2)}) %copy-start.9) | copy-done | bytes 8388632
  177.8 0.0 copy-start.11
  177.8 1.2 copy-done.11
  179.0 8.7 %weight_part.1.part = bf16[4,4,2,256,256]{4,3,2,1,0:T(8,128)(2,1)S(1)} custom-call(bf16[1024,512]{1,0:T(8,128)(2,1)S(1)} %copy-done.11, bf16[1024,4096]{1,0:T(8,128)(2,1)S(1)} %copy-done.9), custom_call_target="tpu_custom_call" | custom-call | flops 4294967296 | bytes 14680064 | tf_op jit(solution)/shard_map/weight_part/pallas_call | solution.py:343
  187.8 0.0 copy-start
  187.8 1.9 copy-done
  189.7 0.0 copy-start.1
  189.7 2.2 copy-done.1
  191.9 50.6 %return_grads.1 = (bf16[128,4096]{1,0:T(8,128)(2,1)S(1)}, bf16[128,4096]{1,0:T(8,128)(2,1)S(1)}, bf16[128,4096]{1,0:T(8,128)(2,1)S(1)}, f32[256,256]{1,0:T(8,128)S(1)}) custom-call(bf16[3,2,1024,256]{3,2,1,0:T(8,128)(2,1)S(1)} %get-tuple-element.41.grad, bf16[4,4,2,256,256]{4,3,2,1,0:T(8,128)(2,1)S(1)} %copy-done.1), custom_call_target="tpu_custom_call" | custom-call | tf_op jit(solution)/shard_map/return_grads/pallas_call | solution.py:536
  242.5 0.0 copy-start.2
  242.5 1.0 copy-done.2
  243.5 0.0 copy-start.4
  243.5 1.0 copy-done.4
  244.5 0.0 copy-start.5
  244.5 1.0 copy-done.5
  245.5 0.0 copy-start.3
  245.5 69.4 %all-reduce.4.cloned.1.call-done = (f32[24,512]{1,0:T(8,128)}, f32[32,256]{1,0:T(8,128)}) async-done(((f32[24,512]{1,0:T(8,128)}, f32[32,256]{1,0:T(8,128)}), (f32[24,512]{1,0:T(8,128)}, f32[32,256]{1,0:T(8,128)})) %all-reduce.4.cloned.1.call-update) | async-done | bytes 81936 | tf_op jit(solution)/shard_map/psum | solution.py:576
  314.9 0.7 dynamic-slice_multiply_fusion
  315.6 1.3 fusion.4
  316.9 0.6 slice.29
  317.5 1.4 fusion
  318.9 2.3 copy.21
  321.2 2.3 copy.22
  323.5 0.0 copy-done.3
  323.5 1.0 copy.23
  324.4 0.7 copy.24
  (7 shorter events, 0.0 us)
Async XLA Ops:
  7.2 307.7 %all-reduce.4.cloned.1.call-start = ((), (), s32[]{:S(2)}) async-start(), calls=%async_computation | async-start | bytes 163840 | tf_op jit(solution)/shard_map/psum | solution.py:576
  97.2 8.3 %copy-start.6 = (f32[2,2,16,256]{3,2,1,0:T(8,128)S(1)}, f32[2,2,16,256]{3,2,1,0:T(8,128)}, u32[]{:S(2)}) copy-start(f32[2,2,16,256]{3,2,1,0:T(8,128)} %get-tuple-element.32.revs.fwds) | copy-start | bytes 196612
  97.2 8.3 %copy-start.7 = (f32[2,3,7,256]{3,2,1,0:T(8,128)S(1)}, f32[2,3,7,256]{3,2,1,0:T(8,128)}, u32[]{:S(2)}) copy-start(f32[2,3,7,256]{3,2,1,0:T(8,128)} %get-tuple-element.31.taps) | copy-start | bytes 129028
  97.2 8.3 %copy-start.8 = (f32[2,1,256]{2,1,0:T(1,128)S(1)}, f32[2,1,256]{2,1,0:T(1,128)}, u32[]{:S(2)}) copy-start(f32[2,1,256]{2,1,0:T(1,128)} %get-tuple-element.33.gain) | copy-start | bytes 6148
  131.0 1.0 copy-start.10
  132.0 18.6 %collective-permute-start = (bf16[192,512]{1,0:T(8,128)(2,1)S(1)}, bf16[192,512]{1,0:T(8,128)(2,1)S(1)}, u32[]{:S(2)}, u32[]{:S(2)}) collective-permute-start(bf16[192,512]{1,0:T(8,128)(2,1)S(1)} %pad_maximum_fusion), channel_id=1, source_target_pairs={{8,0},{16,8},{24,16},{32,24},{40,32},{48,40},{56,48},{64,56},{72,6... | collective-permute-start | bytes 589832 | tf_op jit(solution)/shard_map/ppermute | solution.py:573
  174.4 3.4 %copy-start.9 = (bf16[1024,4096]{1,0:T(8,128)(2,1)S(1)}, bf16[1024,4096]{1,0:T(8,128)(2,1)}, u32[]{:S(2)}) copy-start(bf16[1024,4096]{1,0:T(8,128)(2,1)} %get-tuple-element.29.cot) | copy-start | bytes 25165828
  177.8 1.2 copy-start.11
  187.8 1.9 copy-start
  189.7 2.2 copy-start.1
  242.5 1.0 copy-start.2
  243.5 1.0 copy-start.4
  244.5 1.0 copy-start.5
  245.5 78.0 %copy-start.3 = (bf16[128,4096]{1,0:T(8,128)(2,1)S(1)}, bf16[128,4096]{1,0:T(8,128)(2,1)}, u32[]{:S(2)}) copy-start(bf16[128,4096]{1,0:T(8,128)(2,1)} %copy-done.2) | copy-start | bytes 3145732
Sparse Core Ops, SparseCore 0:
  174.5 140.2 all-reduce.3

commit v2 on v1

--- a/solution.py
+++ b/solution.py
@@ -260,11 +260,11 @@
         r = HALO + 64 * b
         here = pl.multiple_of(64 * b, 64)
         one, two = feature(1, r, 64), feature(2, r, 64)
-        f1_o[pl.ds(here, 64), :] = one.astype(jnp.bfloat16)
-        f2_o[pl.ds(here, 64), :] = two.astype(jnp.bfloat16)
+        f1_o[0, pl.ds(here, 64), :] = one.astype(jnp.bfloat16)
+        f2_o[0, pl.ds(here, 64), :] = two.astype(jnp.bfloat16)
         both = one * two
         prod[pl.ds(here + 128, 64), :] = both
-        p_o[pl.ds(here, 64), :] = both.astype(jnp.bfloat16)
+        p_o[0, pl.ds(here, 64), :] = both.astype(jnp.bfloat16)
 
     lane = lax.broadcasted_iota(jnp.int32, (16, 128), 1)
 
@@ -294,9 +294,9 @@
             lead = feature(0, HALO + 128 * b + r, 16)
             back = mg[here, :]
             mix_o[here, :] = (lead * whole).astype(jnp.bfloat16)
-            qf_o[here, :] = (back * whole).astype(jnp.bfloat16)
+            qf_o[0, here, :] = (back * whole).astype(jnp.bfloat16)
             slope = back * lead
-            sl_o[here, :] = slope.astype(jnp.bfloat16)
+            sl_o[0, here, :] = slope.astype(jnp.bfloat16)
             slopes.append(slope)
         slopes = spread(slopes, lane)
         for g in range(8):
@@ -309,7 +309,7 @@
     return pl.pallas_call(
         forward_kernel,
         grid=(4,),
-        out_shape=(bf(1024, 512),) * 6 + (bf(32, 256, 128), bf(32, 128, 128)),
+        out_shape=(bf(4, 1024, 128),) * 5 + (bf(1024, 512),) + (bf(32, 256, 128), bf(32, 128, 128)),
         in_specs=[
             pl.BlockSpec((3, 1, 1024 + HALO, 128), lambda p: (0, p // 2, 0, p % 2)),
             nat,
@@ -317,7 +317,7 @@
             pl.BlockSpec((1, 1, 8, 256), lambda p: (p // 2, 0, p % 2, 0)),
             pl.BlockSpec((1, 1, 128), lambda p: (p // 2, 0, p % 2)),
         ],
-        out_specs=(nat,) * 6 + (pl.BlockSpec((8, 256, 128), lambda p: (p, 0, 0)), pl.BlockSpec((8, 128, 128), lambda p: (p, 0, 0))),
+        out_specs=(pl.BlockSpec((1, 1024, 128), lambda p: (p, 0, 0)),) * 5 + (nat,) + (pl.BlockSpec((8, 256, 128), lambda p: (p, 0, 0)), pl.BlockSpec((8, 128, 128), lambda p: (p, 0, 0))),
         scratch_shapes=[
             pltpu.VMEM((3, 1024 + HALO, 128), jnp.float32),
             pltpu.VMEM((1152, 128), jnp.float32),
@@ -353,163 +353,151 @@
     )(mix, cot)
 
 
-def backward_kernel(ext, dg, pg, sl, p, f1, f2, qf, edge, taps, fwds, gain, grad_o, short_o, long_o, stage, feat, group):
-    zl, y, zh, _, _ = place()
-    started = 8 * zl + 2 * y + zh > 0
-    for i in range(3):
-        lead = ext[i, 0, HALO - 16 : HALO, :].astype(jnp.float32)
-        stage[i, 0:16, :] = jnp.where(started, lead, 0.0)
-
-    @pl.loop(0, 8)
-    def _(b):
-        for i in range(3):
-            stage[i, pl.ds(pl.multiple_of(16 + 128 * b, 16), 128), :] = ext[i, 0, pl.ds(pl.multiple_of(HALO + 128 * b, 16), 128), :].astype(jnp.float32)
-
-    wide = lax.broadcasted_iota(jnp.int32, (128, 128), 1)
-    lane = lax.broadcasted_iota(jnp.int32, (16, 128), 1)
-    after = edge[0:128, :].astype(jnp.float32)
-    tail = jnp.concatenate([edge[0:HALO, :], jnp.zeros((256 - HALO, 128), jnp.bfloat16)], 0)
-    over = jnp.zeros((16, 128), jnp.float32)
-    square = [lax.broadcasted_iota(jnp.int32, (256, 256), a) for a in (0, 1)]
-    flip = (square[0] + square[1] == 255).astype(jnp.bfloat16)
-    for g in range(8):
-        table = pltpu.roll(jnp.broadcast_to(fwds[0, 0, g : g + 1, :], (128, 256)), 0, 1, stride=1, stride_axis=0).astype(jnp.bfloat16)
-        here = dg[g]
-        head = after if g == 7 else pltpu.roll(after, 16 * (7 - g), 1)
-        later = jnp.where(wide >= 112, head, pltpu.roll(here.astype(jnp.float32), 112, 1)).astype(jnp.bfloat16)
-        group[g] = jnp.dot(table[:, :128], here, preferred_element_type=jnp.float32) + jnp.dot(table[:, 128:], later, preferred_element_type=jnp.float32)
-        past = jnp.dot(table[:16], tail, preferred_element_type=jnp.float32)
-        over = jnp.where(lane // 16 == g, past, over)
-        back = jnp.dot(flip, pg[g], preferred_element_type=jnp.float32).astype(jnp.bfloat16)
-        gram = lax.dot_general(here, back, (((1,), (1,)), ((), ())), preferred_element_type=jnp.float32)
-        lined = pltpu.roll(gram, 0, 1, stride=1, stride_axis=0)
-        long_o[g : g + 1, :] = jnp.sum(lined, axis=0, keepdims=True)
-
-    def gain_sum(m, total):
-        r = pl.multiple_of(16 * m, 16)
-        back = spread([group[g, pl.ds(r, 16), :] for g in range(8)], lane)
-        for b in range(8):
-            here = pl.ds(pl.multiple_of(128 * b + r, 16), 16)
-            slope = sl[here, :].astype(jnp.float32)
-            whole = back[b] + gain[0] * slope
-            feat[0, here, :] = qf[here, :].astype(jnp.float32)
-            feat[1, here, :] = whole * f2[here, :].astype(jnp.float32)
-            feat[2, here, :] = whole * f1[here, :].astype(jnp.float32)
-            term = slope * p[here, :].astype(jnp.float32)
-            total = total + term[:8] + term[8:]
-        return total
-
-    total = lax.fori_loop(0, 8, gain_sum, jnp.zeros((8, 128), jnp.float32))
-    over = over + gain[0] * edge[0:16, :].astype(jnp.float32)
-    feat[0, 1024:1040, :] = edge[HALO + 32 : HALO + 48, :].astype(jnp.float32)
-    feat[1, 1024:1040, :] = over * edge[HALO + 16 : HALO + 32, :].astype(jnp.float32)
-    feat[2, 1024:1040, :] = over * edge[HALO : HALO + 16, :].astype(jnp.float32)
-
-    for i in range(3):
-
-        def rows_sum(b, sums):
-            r = 64 * b
-            grad = taps[0, i, 0:1, :] * feat[i, pl.ds(r, 64), :]
-            for j in range(1, SHORT):
-                grad = grad + taps[0, i, j : j + 1, :] * feat[i, pl.ds(r + j, 64), :]
-            grad_o[i, 0, pl.ds(pl.multiple_of(r, 64), 64), :] = grad.astype(jnp.bfloat16)
-            mine = feat[i, pl.ds(r, 64), :]
-            out = []
-            for j in range(SHORT):
-                term = mine * stage[i, pl.ds(16 + r - j, 64), :]
-                out.append(sums[j] + jnp.sum(term.reshape(8, 8, 128), axis=0))
-            return tuple(out)
-
-        sums = lax.fori_loop(0, 16, rows_sum, (jnp.zeros((8, 128), jnp.float32),) * SHORT)
-        for j in range(SHORT):
-            short_o[8 * i + j : 8 * i + j + 1, :] = jnp.sum(sums[j], axis=0, keepdims=True)
-        short_o[8 * i + SHORT : 8 * i + 8, :] = jnp.sum(total, axis=0, keepdims=True)
-
-
-def backward(ext, dg, pg, sl, p, f1, f2, qf, edge, taps, fwds, gain):
-    nat = pl.BlockSpec((1024, 128), lambda q: (0, q))
-    return pl.pallas_call(
-        backward_kernel,
-        grid=(4,),
-        out_shape=(
-            jax.ShapeDtypeStruct((3, 2, 1024, 256), jnp.bfloat16),
-            jax.ShapeDtypeStruct((24, 512), jnp.float32),
-            jax.ShapeDtypeStruct((32, 256), jnp.float32),
-        ),
-        in_specs=[
-            pl.BlockSpec((3, 1, 1024 + HALO, 128), lambda q: (0, q // 2, 0, q % 2)),
-            pl.BlockSpec((8, 128, 128), lambda q: (q, 0, 0)),
-            pl.BlockSpec((8, 256, 128), lambda q: (q, 0, 0)),
-        ]
-        + [nat] * 5
-        + [
-            pl.BlockSpec((HALO + 48, 128), lambda q: (0, q)),
-            pl.BlockSpec((1, 3, SHORT, 128), lambda q: (q // 2, 0, 0, q % 2)),
-            pl.BlockSpec((1, 1, 8, 256), lambda q: (q // 2, 1, q % 2, 0)),
-            pl.BlockSpec((1, 1, 128), lambda q: (q // 2, 0, q % 2)),
-        ],
-        out_specs=(
-            pl.BlockSpec((3, 1, 1024, 128), lambda q: (0, q // 2, 0, q % 2)),
-            pl.BlockSpec((24, 128), lambda q: (0, q)),
-            pl.BlockSpec((8, 256), lambda q: (q, 0)),
-        ),
-        scratch_shapes=[
-            pltpu.VMEM((3, 1024 + 16, 128), jnp.float32),
-            pltpu.VMEM((3, 1024 + 16, 128), jnp.float32),
-            pltpu.VMEM((8, 128, 128), jnp.float32),
-        ],
-        compiler_params=pltpu.CompilerParams(vmem_limit_bytes=40 * 2**20),
-        name="mixer_backward",
-    )(ext, dg, pg, sl, p, f1, f2, qf, edge, taps, fwds, gain)
-
-
-def return_kernel(grad, part, gq, gk, gv, wout, mine, land, once, zland, a2a_s, a2a_r, own, wy_s, wy_r, wz_s, wz_r):
+def backward_kernel(
+    ext, dg, pg, sl, p, f1, f2, qf, edge, part, taps, tabs, gain,
+    gq, gk, gv, wout, small_o,
+    ext_v, dg_v, pg_v, sl_v, p_v, f1_v, f2_v, qf_v, edge_v, grad, stage, feat, group, small,
+    mine, land, once, zland, small_y, small_t, small_z,
+    load, own, a2a_s, a2a_r, wy_s, wy_r, wz_s, wz_r, sy_s, sy_r, sz_s, sz_r,
+):
     zl, y, zh, x, c = place()
     s = 2 * x + c
     zpos = 4 * zh + zl
+    started = 8 * zl + 2 * y + zh > 0
     greet([group_peer(o) for o in range(1, 8)] + [z_peer(o) for o in range(1, 8)] + [y_peer(o) for o in range(1, 4)])
-    order = (4, 3, 5, 2, 6, 1, 7, 0)
-
+
+    def loads(q):
+        cols = pl.ds(pl.multiple_of(128 * lax.rem(q, 2), 128), 128)
+        pairs = [(ext.at[:, q // 2, HALO - 16 : HALO + 1024, cols], ext_v.at[q])]
+        pairs += [(dg.at[pl.ds(8 * q, 8)], dg_v.at[pl.ds(8 * q, 8)]), (pg.at[pl.ds(8 * q, 8)], pg_v.at[pl.ds(8 * q, 8)])]
+        pairs += [(a.at[q], b.at[q]) for a, b in ((sl, sl_v), (p, p_v), (f1, f1_v), (f2, f2_v), (qf, qf_v), (edge, edge_v))]
+        return [pltpu.make_async_copy(a, b, load.at[q, n]) for n, (a, b) in enumerate(pairs)]
+
+    for cp in loads(0):
+        cp.start()
     fetch = pltpu.make_async_copy(part.at[y], mine, own)
     fetch.start()
-    to_y = []
-    for k in order:
+    for k in range(7, -1, -1):
         t = lax.rem(zpos + k, 8)
         for o in range(1, 4):
-            cp = remote(
+            remote(
                 part.at[lax.rem(y + o, 4), lax.rem(t, 4), t // 4], land.at[o - 1, k], wy_s.at[o - 1, k], wy_r.at[o - 1, k], y_peer(o)
-            )
+            ).start()
+    for q in range(1, 4):
+        for cp in loads(q):
             cp.start()
-            to_y.append(cp)
-    for o in (2, 6, 3, 5, 4, 7, 1, 0):
-        d = lax.rem(s + o, 8)
-        for slab in range(2):
-            cols = pl.ds(pl.multiple_of(2048 * slab + 256 * s, 256), 256)
+    fetch.wait()
+
+    wide = lax.broadcasted_iota(jnp.int32, (128, 128), 1)
+    lane = lax.broadcasted_iota(jnp.int32, (16, 128), 1)
+    square = [lax.broadcasted_iota(jnp.int32, (256, 256), a) for a in (0, 1)]
+
+    @pl.loop(0, 4)
+    def _(q):
+        slab, half = q // 2, lax.rem(q, 2)
+        cols = pl.ds(pl.multiple_of(128 * half, 128), 128)
+        for cp in loads(q):
+            cp.wait()
+        for i in range(3):
+            lead = ext_v[q, i, 0:16, :].astype(jnp.float32)
+            stage[i, 0:16, :] = jnp.where(started, lead, 0.0)
+
+        @pl.loop(0, 8)
+        def _(b):
+            here = pl.ds(pl.multiple_of(16 + 128 * b, 16), 128)
+            for i in range(3):
+                stage[i, here, :] = ext_v[q, i, here, :].astype(jnp.float32)
+
+        skip = gain[slab, 0:1, cols]
+        flip = (square[0] + square[1] == 255).astype(jnp.bfloat16)
+        after = edge_v[q, 0:128, :].astype(jnp.float32)
+        tail = jnp.concatenate([edge_v[q, 0:HALO, :], jnp.zeros((256 - HALO, 128), jnp.bfloat16)], 0)
+        over = jnp.zeros((16, 128), jnp.float32)
+        for g in range(8):
+            row = tabs[slab, 1, pl.ds(8 * half + g, 1), :]
+            table = pltpu.roll(jnp.broadcast_to(row, (128, 256)), 0, 1, stride=1, stride_axis=0).astype(jnp.bfloat16)
+            here = dg_v[8 * q + g]
+            head = after if g == 7 else pltpu.roll(after, 16 * (7 - g), 1)
+            later = jnp.where(wide >= 112, head, pltpu.roll(here.astype(jnp.float32), 112, 1)).astype(jnp.bfloat16)
+            group[g] = jnp.dot(table, jnp.concatenate([here, later], 0), preferred_element_type=jnp.float32)
+            past = jnp.dot(table[:16], tail, preferred_element_type=jnp.float32)
+            over = jnp.where(lane // 16 == g, past, over)
+            back = jnp.dot(flip, pg_v[8 * q + g], preferred_element_type=jnp.float32).astype(jnp.bfloat16)
+            gram = lax.dot_general(here, back, (((1,), (1,)), ((), ())), preferred_element_type=jnp.float32)
+            lined = pltpu.roll(gram, 0, 1, stride=1, stride_axis=0)
+            small[slab, pl.ds(24 + 8 * half + g, 1), :] = jnp.sum(lined, axis=0, keepdims=True)
+
+        def gain_sum(m, total):
+            r = pl.multiple_of(16 * m, 16)
+            back = spread([group[g, pl.ds(r, 16), :] for g in range(8)], lane)
+            for b in range(8):
+                here = pl.ds(pl.multiple_of(128 * b + r, 16), 16)
+                slope = sl_v[q, here, :].astype(jnp.float32)
+                whole = back[b] + skip * slope
+                feat[0, here, :] = qf_v[q, here, :].astype(jnp.float32)
+                feat[1, here, :] = whole * f2_v[q, here, :].astype(jnp.float32)
+                feat[2, here, :] = whole * f1_v[q, here, :].astype(jnp.float32)
+                term = slope * p_v[q, here, :].astype(jnp.float32)
+                total = total + term[:8] + term[8:]
+            return total
+
+        total = lax.fori_loop(0, 8, gain_sum, jnp.zeros((8, 128), jnp.float32))
+        over = over + skip * edge_v[q, 0:16, :].astype(jnp.float32)
+        feat[0, 1024:1040, :] = edge_v[q, HALO + 32 : HALO + 48, :].astype(jnp.float32)
+        feat[1, 1024:1040, :] = over * edge_v[q, HALO + 16 : HALO + 32, :].astype(jnp.float32)
+        feat[2, 1024:1040, :] = over * edge_v[q, HALO : HALO + 16, :].astype(jnp.float32)
+
+        for i in range(3):
+            tap = [taps[slab, i, j : j + 1, cols] for j in range(SHORT)]
+
+            def rows_sum(b, sums):
+                r = pl.multiple_of(64 * b, 64)
+                mine_ = feat[i, pl.ds(r, 64), :]
+                total_ = tap[0] * mine_
+                for j in range(1, SHORT):
+                    total_ = total_ + tap[j] * feat[i, pl.ds(r + j, 64), :]
+                grad[i, slab, pl.ds(r, 64), cols] = total_.astype(jnp.bfloat16)
+                out = []
+                for j in range(SHORT):
+                    term = mine_ * stage[i, pl.ds(16 + r - j, 64), :]
+                    out.append(sums[j] + jnp.sum(term.reshape(8, 8, 128), axis=0))
+                return tuple(out)
+
+            sums = lax.fori_loop(0, 16, rows_sum, (jnp.zeros((8, 128), jnp.float32),) * SHORT)
+            for j in range(SHORT):
+                small[slab, 8 * i + j : 8 * i + j + 1, cols] = jnp.sum(sums[j], axis=0, keepdims=True)
+            small[slab, 8 * i + SHORT : 8 * i + 8, cols] = jnp.sum(total, axis=0, keepdims=True)
+
+        for o in (2, 6, 3, 5, 4, 7, 1, 0):
+            d = lax.rem(s + o, 8)
+            to = pl.ds(pl.multiple_of(2048 * slab + 256 * s + 128 * half, 128), 128)
             for i, dst in enumerate((gq, gk, gv)):
-                src = grad.at[i, slab, pl.ds(pl.multiple_of(128 * d, 128), 128), :]
+                src = grad.at[i, slab, pl.ds(pl.multiple_of(128 * d, 128), 128), cols]
                 if o:
-                    remote(src, dst.at[:, cols], a2a_s.at[o], a2a_r.at[o], group_peer(o)).start()
+                    remote(src, dst.at[:, to], a2a_s.at[q, o], a2a_r.at[q, o], group_peer(o)).start()
                 else:
-                    pltpu.make_async_copy(src, dst.at[:, cols], a2a_s.at[0]).start()
-    fetch.wait()
-    to_z = []
-    for k in order:
-        t = lax.rem(zpos + k, 8)
-        for o in range(3):
-            landed(land.at[o, k], wy_r.at[o, k])
-
-        @pl.loop(0, 4)
-        def _(n):
-            rows = pl.ds(pl.multiple_of(64 * n, 64), 64)
-            total = mine[lax.rem(t, 4), t // 4, rows, :].astype(jnp.float32)
+                    pltpu.make_async_copy(src, dst.at[:, to], a2a_s.at[q, 0]).start()
+
+        for m in range(2):
+            k = 7 - 2 * q - m
+            t = lax.rem(zpos + k, 8)
             for o in range(3):
-                total = total + land[o, k, rows, :].astype(jnp.float32)
-            once[k, rows, :] = total.astype(jnp.bfloat16)
-
-        if k:
-            cp = remote(once.at[k], zland.at[k], wz_s.at[k], wz_r.at[k], z_peer(k))
-            cp.start()
-            to_z.append(cp)
+                landed(land.at[o, k], wy_r.at[o, k])
+
+            @pl.loop(0, 4)
+            def _(n):
+                rows = pl.ds(pl.multiple_of(64 * n, 64), 64)
+                total = mine[lax.rem(t, 4), t // 4, rows, :].astype(jnp.float32)
+                for o in range(3):
+                    total = total + land[o, k, rows, :].astype(jnp.float32)
+                once[k, rows, :] = total.astype(jnp.bfloat16)
+
+            @pl.when(k > 0)
+            def _():
+                remote(once.at[k], zland.at[k], wz_s.at[k], wz_r.at[k], z_peer(k)).start()
+
+    for o in range(1, 4):
+        remote(small, small_y.at[o - 1], sy_s.at[o - 1], sy_r.at[o - 1], y_peer(o)).start()
     for k in range(1, 8):
         landed(zland.at[k], wz_r.at[k])
 
@@ -521,39 +509,58 @@
             total = total + zland[k, rows, :].astype(jnp.float32)
         wout[rows, :] = total * SCALE
 
-    for cp in to_y + to_z:
-        cp.wait_send()
-    six = grad.at[:, :, 0:128, :]
-    for o in range(8):
-        landed(six, a2a_s.at[o])
-        if o:
-            landed(six, a2a_r.at[o])
-
-
-def give_back(grad, part):
+    for o in range(3):
+        landed(small, sy_r.at[o])
+    small_t[...] = small[...] + small_y[0] + small_y[1] + small_y[2]
+    for k in range(1, 8):
+        t = lax.rem(zpos + k, 8)
+        remote(small_t.at[t // 4], small_z.at[k], sz_s.at[k], sz_r.at[k], z_peer(k)).start()
+    for k in range(1, 8):
+        landed(small_z.at[k], sz_r.at[k])
+    total = small_t[zh]
+    for k in range(1, 8):
+        total = total + small_z[k]
+    small_o[...] = total * SCALE
+
+    for o in range(3):
+        landed(small, sy_s.at[o])
+        for k in range(8):
+            landed(land.at[o, k], wy_s.at[o, k])
+    for k in range(1, 8):
+        landed(once.at[k], wz_s.at[k])
+        landed(small_z.at[k], sz_s.at[k])
+    piece = grad.at[:, 0, 0:128, 0:128]
+    for q in range(4):
+        for o in range(8):
+            landed(piece, a2a_s.at[q, o])
+            if o:
+                landed(piece, a2a_r.at[q, o])
+
+
+def backward(ext, dg, pg, sl, p, f1, f2, qf, edge, part, taps, tabs, gain):
     dma = pltpu.SemaphoreType.DMA
     tok = jax.ShapeDtypeStruct((128, 4096), jnp.bfloat16)
+    vmem = pl.BlockSpec(memory_space=pltpu.VMEM)
+    bf = lambda *shape: pltpu.VMEM(shape, jnp.bfloat16)
+    f32 = lambda *shape: pltpu.VMEM(shape, jnp.float32)
     return pl.pallas_call(
-        return_kernel,
-        out_shape=(tok, tok, tok, jax.ShapeDtypeStruct((256, 256), jnp.float32)),
-        in_specs=[ANY] * 2,
-        out_specs=(ANY,) * 3 + (pl.BlockSpec(memory_space=pltpu.VMEM),),
+        backward_kernel,
+        out_shape=(tok, tok, tok, jax.ShapeDtypeStruct((256, 256), jnp.float32), jax.ShapeDtypeStruct((40, 256), jnp.float32)),
+        in_specs=[ANY] * 10 + [vmem] * 3,
+        out_specs=(ANY,) * 3 + (vmem,) * 2,
         scratch_shapes=[
-            pltpu.VMEM((4, 2, 256, 256), jnp.bfloat16),
-            pltpu.VMEM((3, 8, 256, 256), jnp.bfloat16),
-            pltpu.VMEM((8, 256, 256), jnp.bfloat16),
-            pltpu.VMEM((8, 256, 256), jnp.bfloat16),
-            dma((8,)),
-            dma((8,)),
-            dma,
-            dma((3, 8)),
-            dma((3, 8)),
-            dma((8,)),
-            dma((8,)),
+            bf(4, 3, 1024 + 16, 128), bf(32, 128, 128), bf(32, 256, 128),
+            bf(4, 1024, 128), bf(4, 1024, 128), bf(4, 1024, 128), bf(4, 1024, 128), bf(4, 1024, 128),
+            bf(4, HALO + 48, 128), bf(3, 2, 1024, 256),
+            f32(3, 1024 + 16, 128), f32(3, 1024 + 16, 128), f32(8, 128, 128), f32(2, 40, 256),
+            bf(4, 2, 256, 256), bf(3, 8, 256, 256), bf(8, 256, 256), bf(8, 256, 256),
+            f32(3, 2, 40, 256), f32(2, 40, 256), f32(8, 40, 256),
+            dma((4, 9)), dma, dma((4, 8)), dma((4, 8)), dma((3, 8)), dma((3, 8)), dma((8,)), dma((8,)),
+            dma((3,)), dma((3,)), dma((8,)), dma((8,)),
         ],
-        compiler_params=pltpu.CompilerParams(collective_id=1, has_side_effects=True, vmem_limit_bytes=40 * 2**20),
-        name="return_grads",
-    )(grad, part)
+        compiler_params=pltpu.CompilerParams(collective_id=1, has_side_effects=True, vmem_limit_bytes=48 * 2**20),
+        name="mixer_backward",
+    )(ext, dg, pg, sl, p, f1, f2, qf, edge, part, taps, tabs, gain)
 
 
 def body(q, k, v, cot, w, short_taps, long_taps, skip_gain):
@@ -568,17 +575,12 @@
     ext, cotg, wg, taps, tables, gain = gather(q, k, v, cot, w, short_taps, tables, skip_gain[None, :])
     mg = lax.dot_general(cotg, wg, (((1,), (1,)), ((), ())), preferred_element_type=jnp.float32)
     f1, f2, p, qf, sl, mix, pg, dg = forward(ext, mg, taps, tables, gain)
-    edge = jnp.concatenate([sl[:HALO], f1[:16], f2[:16], qf[:16]], 0)
+    edge = jnp.concatenate([sl[:, :HALO], f1[:, :16], f2[:, :16], qf[:, :16]], 1)
     route = [(i + 1, i) for i in range(31)]
     edge = lax.ppermute(edge, ("zl", "y", "zh"), route)
     part = weight_part(mix, cotg)
-    grad, short, long = backward(ext, dg, pg, sl, p, f1, f2, qf, edge, taps, tables, gain)
-    short, long = lax.psum((short, long), ("zl", "y", "zh"))
-    gq, gk, gv, wout = give_back(grad, part)
-    zh = lax.axis_index("zh")
-    short = lax.dynamic_slice_in_dim(short, 256 * zh, 256, 1) * SCALE
-    long = lax.dynamic_slice_in_dim(long, 16 * zh, 16, 0)[:, 127:255].T * SCALE
-    return gq, gk, gv, wout, short.reshape(3, 8, 256)[:, :SHORT], long, short[SHORT]
+    gq, gk, gv, wout, small = backward(ext, dg, pg, sl, p, f1, f2, qf, edge, part, taps, tables, gain)
+    return gq, gk, gv, wout, small[:24].reshape(3, 8, 256)[:, :SHORT], small[24:, 127:255].T, small[SHORT]
 
 
 def solution(mesh):

time: 333 us -> 219 us (0.66)
  waiting for transfers between devices: 86.7 us -> 6.56 us
  between operations: 14.2 us -> 0.86 us
  local copies, waits for them, and re-layouts: 20.3 us -> 10.7 us
  Pallas kernels: 196 us -> 188 us
  other arithmetic: 4.89 us -> 1.41 us
    psum x1 -> x0, waiting for transfers between devices: 69.4 us -> none  [body(): short, long = lax.psum((short, long), ('zl', 'y', 'zh'))]
    unnamed x28 -> x26, local copies, waits for them, and re-layouts: 18.9 us -> 7.94 us
    ppermute x1, waiting for transfers between devices: 17.3 us -> 6.56 us  [body(): edge = lax.ppermute(edge, ('zl', 'y', 'zh'), route)]
    pallas_call x3 -> x2, Pallas kernels: 99.8 us -> 91.7 us  [the longest x1 67.2 us: backward(): pl.pallas_call(backward_kernel, out_shape=(tok, tok, tok, jax.ShapeDtypeS...]
  transfers between devices with their start and end apart: 2 -> 1, of which waited for: 2 -> 1; matrix products, arithmetic and copies ran while one was open for 0% -> 0% of each run, Pallas kernels for 18% -> 4%
where the time goes in v2:
time: 219 us; the launch traced here: 217 us
  Pallas kernels  188 us (86%)
  local copies, waits for them, and re-layouts  10.7 us (5%)
  matrix products  8.36 us (4%)
  waiting for transfers between devices  6.56 us (3%)
    pallas_call x1, Pallas kernels, gather(): pl.pallas_call(gather_kernel, out_shape=(jax.ShapeDtypeStruct((3, 2, 1024...  87.7 us
    pallas_call x1, Pallas kernels, backward(): pl.pallas_call(backward_kernel, out_shape=(tok, tok, tok, jax.ShapeDtypeS...  67.2 us
    pallas_call x1, Pallas kernels, forward(): pl.pallas_call(forward_kernel, grid=(4,), out_shape=(bf(4, 1024, 128),) *...  24.5 us
    pallas_call x1, Pallas kernels, weight_part(): pl.pallas_call(weight_kernel, grid=(16,), out_shape=jax.ShapeDtypeStruct(...  8.75 us
    dot_general x1, matrix products, body(): lax.dot_general(cotg, wg, (((1,), (1,)), ((), ())), preferred_element_typ...  8.36 us
    unnamed x26, local copies, waits for them, and re-layouts  7.94 us
    ppermute x1, waiting for transfers between devices, body(): edge = lax.ppermute(edge, ('zl', 'y', 'zh'), route)  6.56 us
  transfers between devices with their start and end apart: 1, of which 1 were waited for; matrix products, arithmetic and copies ran while one was open for 0% of the time, Pallas kernels for 4%

profile of v2, /device:TPU:2, one launch (start us, length us, event | category | flops | bytes accessed | tf_op | source)
XLA Modules:
  0.0 217.3 jit_solution(1388208048303926642)
XLA Ops:
  0.6 0.1 pad.9.clone
  0.7 0.8 rev.3
  1.5 0.8 maximum_bitcast_fusion
  2.3 0.6 pad_maximum_fusion.1.tabs
  2.9 87.7 %gather_inputs.1 = (bf16[3,2,1168,256]{3,2,1,0:T(8,128)(2,1)}, bf16[1024,4096]{1,0:T(8,128)(2,1)}, bf16[512,4096]{1,0:T(8,128)(2,1)}, f32[2,3,7,256]{3,2,1,0:T(8...) custom-call(bf16[128,4096]{1,0:T(8,128)(2,1)} %q.1, bf16[128,4096]{1,0:T(8,128)(2,1)} %k.1, bf16[128,4096]{1,0:T(8,128)(2,1)} %v.1, ...), custom_call_target="tpu_custom_call" | custom-call | tf_op jit(solution)/shard_map/gather_inputs/pallas_call | solution.py:203
  90.6 0.0 slice-start
  90.6 0.0 copy-start.6
  90.7 0.0 copy-start.7
  90.7 0.0 copy-start.8
  90.7 0.0 slice-start.1
  90.7 8.4 %fusion.mg = f32[1024,512]{1,0:T(8,128)S(1)} fusion(bf16[1024,4096]{1,0:T(8,128)(2,1)} %get-tuple-element.27.cot, bf16[512,4096]{1,0:T(8,128)(2,1)} %get-tuple-element.28), kind=kOutput, calls=%fused_computation.6 | convolution fusion | flops 4294967296 | bytes 14680064 | tf_op jit(solution)/shard_map/dot_general | solution.py:576
  99.0 0.0 copy-done.6
  99.1 0.0 copy-done.7
  99.1 0.0 copy-done.8
  99.1 24.5 %mixer_forward.1 = (bf16[4,1024,128]{2,1,0:T(8,128)(2,1)S(1)}, bf16[4,1024,128]{2,1,0:T(8,128)(2,1)S(1)}, bf16[4,1024,128]{2,1,0:T(8,128)(2,1)S(1)}, bf16[4,1024...) custom-call(bf16[3,2,1168,256]{3,2,1,0:T(8,128)(2,1)} %get-tuple-ele, ...), custom_call_target="tpu_custom_call" | custom-call | tf_op jit(solution)/shard_map/mixer_forward/pallas_call | solution.py:309
  123.6 0.0 copy-start.1
  123.6 1.4 copy-done.1
  125.0 0.0 copy-start.5
  125.0 1.0 copy-done.5
  126.0 0.0 copy-start.2
  126.0 0.0 copy-start.3
  126.0 0.0 copy-start.4
  126.0 1.3 collective-permute-start
  127.3 0.0 slice-done
  127.4 0.0 slice-done.1
  127.4 8.7 %weight_part.1.part = bf16[4,4,2,256,256]{4,3,2,1,0:T(8,128)(2,1)S(1)} custom-call(bf16[1024,512]{1,0:T(8,128)(2,1)S(1)} %get-tuple-element.39.mix, bf16[1024,4096]{1,0:T(8,128)(2,1)S(1)} %bitcast.16), custom_call_target="tpu_custom_call" | custom-call | flops 4294967296 | bytes 14680064 | tf_op jit(solution)/shard_map/weight_part/pallas_call | solution.py:343
  136.1 0.0 copy-done.2
  136.1 0.0 copy-done.3
  136.2 0.0 copy-done.4
  136.2 0.0 copy-start
  136.2 2.0 copy-done
  138.1 6.6 %collective-permute-done.edge = bf16[4,192,128]{2,1,0:T(8,128)(2,1)S(1)} collective-permute-done((bf16[4,192,128]{2,1,0:T(8,128)(2,1)S(1)}, bf16[4,192,128]{2,1,0:T(8,128)(2,1)S(1)}, u32[]{:S(2)}, u32[]{:S(2)}) %collective-permute-start) | collective-permute-done | bytes 196640 | tf_op jit(solution)/shard_map/ppermute | solution.py:580
  144.7 67.2 %mixer_backward.1 = (bf16[128,4096]{1,0:T(8,128)(2,1)S(1)}, bf16[128,4096]{1,0:T(8,128)(2,1)S(1)}, bf16[128,4096]{1,0:T(8,128)(2,1)S(1)}, f32[256,256]{1,0:T(8,128)S(1)}, f32[40,256]{1,0:T(8,128)S(1)}) custom-call(bf16[3,2,1168,256]{3,2,1,0:T(8,128)(2,1)} %get-tuple-element.26.ext, bf16[32,128,128]{2,1,0:T(8,128)(2,1)S(1)} %get-tuple-element.32.dg, ...), custom_call_target="tpu_custom_call" | custom-call | tf_op jit(solution)/shard_map/mixer_backward/pallas_call | solution.py:546
  211.9 0.6 slice.31
  212.4 0.7 slice_bitcast_fusion.1
  213.1 0.6 slice_bitcast_fusion
  213.7 1.0 copy.19
  214.7 1.0 copy.20
  215.7 1.0 copy.21
  216.6 0.7 copy.22
  (8 shorter events, 0.0 us)
Async XLA Ops:
  90.6 36.7 %slice-start = ((s8[8388608]{0:T(1024)(128)(4,1)}), s8[4194304]{0:T(1024)(128)(4,1)S(1)}, s32[]{:S(2)}) async-start(s8[8388608]{0:T(1024)(128)(4,1)} %bitcast.15), calls=%async_computation | async-start | bytes 8388608
  90.6 8.4 %copy-start.6 = (f32[2,2,16,256]{3,2,1,0:T(8,128)S(1)}, f32[2,2,16,256]{3,2,1,0:T(8,128)}, u32[]{:S(2)}) copy-start(f32[2,2,16,256]{3,2,1,0:T(8,128)} %get-tuple-element.30.revs.tabs) | copy-start | bytes 196612
  90.7 8.4 %copy-start.7 = (f32[2,3,7,256]{3,2,1,0:T(8,128)S(1)}, f32[2,3,7,256]{3,2,1,0:T(8,128)}, u32[]{:S(2)}) copy-start(f32[2,3,7,256]{3,2,1,0:T(8,128)} %get-tuple-element.29.taps) | copy-start | bytes 129028
  90.7 8.4 %copy-start.8 = (f32[2,1,256]{2,1,0:T(1,128)S(1)}, f32[2,1,256]{2,1,0:T(1,128)}, u32[]{:S(2)}) copy-start(f32[2,1,256]{2,1,0:T(1,128)} %get-tuple-element.31.gain) | copy-start | bytes 6148
  90.7 36.7 %slice-start.1 = ((s8[8388608]{0:T(1024)(128)(4,1)}), s8[4194304]{0:T(1024)(128)(4,1)S(1)}, s32[]{:S(2)}) async-start(s8[8388608]{0:T(1024)(128)(4,1)} %bitcast.15), calls=%async_computation.1 | async-start | bytes 8388608
  123.6 1.4 copy-start.1
  125.0 1.0 copy-start.5
  126.0 10.2 %copy-start.2 = (bf16[4,1024,128]{2,1,0:T(8,128)(2,1)}, bf16[4,1024,128]{2,1,0:T(8,128)(2,1)S(1)}, u32[]{:S(2)}) copy-start(bf16[4,1024,128]{2,1,0:T(8,128)(2,1)S(1)} %get-tuple-element.36.f1) | copy-start | bytes 3145732
  126.0 10.2 %copy-start.3 = (bf16[4,1024,128]{2,1,0:T(8,128)(2,1)}, bf16[4,1024,128]{2,1,0:T(8,128)(2,1)S(1)}, u32[]{:S(2)}) copy-start(bf16[4,1024,128]{2,1,0:T(8,128)(2,1)S(1)} %get-tuple-element.37.f2) | copy-start | bytes 3145732
  126.0 10.2 %copy-start.4 = (bf16[4,1024,128]{2,1,0:T(8,128)(2,1)}, bf16[4,1024,128]{2,1,0:T(8,128)(2,1)S(1)}, u32[]{:S(2)}) copy-start(bf16[4,1024,128]{2,1,0:T(8,128)(2,1)S(1)} %get-tuple-element.38.qf) | copy-start | bytes 3145732
  126.0 18.6 %collective-permute-start = (bf16[4,192,128]{2,1,0:T(8,128)(2,1)S(1)}, bf16[4,192,128]{2,1,0:T(8,128)(2,1)S(1)}, u32[]{:S(2)}, u32[]{:S(2)}) collective-permute-start(bf16[4,192,128]{2,1,0:T(8,128)(2,1)S(1)} %pad_maximum_fusion), channel_id=1, source_target_pairs={{8,0},{16,8},{24,16},{32,24},{40,32},{48,40},{56,48},{64,56},{72,6... | collective-permute-start | bytes 589832 | tf_op jit(solution)/shard_map/ppermute | solution.py:580
  136.2 2.0 copy-start

commit v3 on v0

v3 whole, which is shorter than its diff:
```python
import functools
import jax
import jax.numpy as jnp
from jax import lax
from jax.experimental import pallas as pl
from jax.experimental.pallas import tpu as pltpu
from jax.sharding import Mesh, PartitionSpec as P

MESH = pl.DeviceIdType.MESH
HALO = 144
SHORT = 7
SCALE = 32768.0 ** -0.5
AXES = ("zl", "y", "zh", "x", "core")


def place():
    return tuple(lax.axis_index(a) for a in AXES)


def group_peer(offset):
    _, _, _, x, c = place()
    s = lax.rem(2 * x + c + offset, 8)
    return {"x": s // 2, "core": lax.rem(s, 2)}


def z_peer(offset):
    zl, _, zh, _, _ = place()
    p = lax.rem(4 * zh + zl + offset, 8)
    return {"zl": lax.rem(p, 4), "zh": p // 4}


def y_peer(offset):
    return {"y": lax.rem(lax.axis_index("y") + offset, 4)}


def x_peer(offset):
    return {"x": lax.rem(lax.axis_index("x") + offset, 4)}


def block_peer(offset):
    zl, y, zh, _, _ = place()
    n = lax.rem(8 * zl + 2 * y + zh + offset, 32)
    return {"zl": n // 8, "y": lax.rem(n // 2, 4), "zh": lax.rem(n, 2)}


def greet(peers):
    barrier = pltpu.get_barrier_semaphore()
    for peer in peers:
        pl.semaphore_signal(barrier, inc=1, device_id=peer, device_id_type=MESH)
    pl.semaphore_wait(barrier, len(peers))


def remote(src, dst, send_sem, recv_sem, peer):
    return pltpu.make_async_remote_copy(
        src_ref=src, dst_ref=dst, send_sem=send_sem, recv_sem=recv_sem, device_id=peer, device_id_type=MESH
    )


def landed(ref, sem):
    pltpu.make_async_copy(ref, ref, sem).wait()


def spread(tiles, lane):
    tiles = list(tiles)
    for k in (1, 2, 4):
        keep = (lane // (16 * k)) % 2 == 0
        for i in range(8):
            if not i & k:
                a, b = tiles[i], tiles[i + k]
                tiles[i] = jnp.where(keep, a, pltpu.roll(b, 16 * k, 1))
                tiles[i + k] = jnp.where(keep, pltpu.roll(a, 128 - 16 * k, 1), b)
    return tiles


def mixer_kernel(
    q, k, v, cot, w, short, tabs, gain,
    gq, gk, gv, wout, small_o,
    ext, cotg, wg, shorts, tabss, gains,
    stage, feat, group, prod, f0, f1, f2, filt, mg, mixed, turned, pgs, dgs, sl, qf, edge_a, edge_b, part, grad, small,
    land, once, zland, small_y, small_t, small_z,
    own, sm_s, sm_r, wz_s, wz_r, wy_s, wy_r, in_s, in_r, halo_s, halo_r, cot_s, cot_r, edge_s, edge_r,
    out_s, out_r, py_s, py_r, pz_s, pz_r, sy_s, sy_r, sz_s, sz_r,
):
    zl, y, zh, x, c = place()
    s = 2 * x + c
    f = 4 * zl + y
    zpos = 4 * zh + zl
    block = 8 * zl + 2 * y + zh
    greet(
        [group_peer(o) for o in range(1, 8)]
        + [z_peer(o) for o in range(1, 8)]
        + [y_peer(o) for o in range(1, 4)]
        + [block_peer(1), block_peer(31)]
    )
    sib = {"core": 1 - c}

    def rows_of(src):
        return pl.ds(pl.multiple_of(HALO + 128 * src, 16), 128)

    def cot_rows(src):
        return cotg.at[pl.ds(pl.multiple_of(128 * src, 128), 128), :]

    def cot_half(src, half):
        return cotg.at[pl.ds(pl.multiple_of(128 * src + 64 * half, 64), 64), :]

    def w_block(zh_, f_):
        return wg.at[pl.ds(pl.multiple_of(256 * zh_, 256), 256), pl.ds(pl.multiple_of(256 * f_, 256), 256)]

    def w_cols(zl_, y_):
        return wg.at[:, pl.ds(pl.multiple_of(1024 * zl_ + 256 * y_, 256), 256)]

    own_w = pltpu.make_async_copy(w, w_block(zh, f), own.at[0])
    own_w.start()
    for o in range(1, 8):
        remote(w, w_block(zh, f), wz_s.at[o], wz_r.at[o], z_peer(o)).start()
    for o in (2, 6, 4, 3, 5, 7, 1, 0):
        d = lax.rem(s + o, 8)
        for slab in range(2):
            cols = pl.ds(pl.multiple_of(2048 * slab + 256 * d, 256), 256)
            for i, src in enumerate((q, k, v)):
                dst = ext.at[i, slab, rows_of(s), :]
                if o:
                    remote(src.at[:, cols], dst, in_s.at[o], in_r.at[o], group_peer(o)).start()
                else:
                    pltpu.make_async_copy(src.at[:, cols], dst, in_s.at[0]).start()
    taps_in = ((short, shorts), (tabs, tabss), (gain, gains))
    for i, (src, dst) in enumerate(taps_in):
        remote(src, dst.at[zh], sm_s.at[i], sm_r.at[i], z_peer(4)).start()
        pltpu.make_async_copy(src, dst.at[zh], own.at[2 + i]).start()
    own_c = pltpu.make_async_copy(cot, cot_rows(s), own.at[1])
    own_c.start()
    remote(cot, cot_rows(s), cot_s.at[2], cot_r.at[2], sib).start()

    own_w.wait()
    landed(w_block(0, 0), wz_r.at[4])
    for zl_ in range(4):
        zl_now = lax.rem(zl + 4 - zl_, 4)
        if zl_:
            landed(w_block(0, 0), wz_r.at[zl_])
            landed(w_block(0, 0), wz_r.at[zl_ + 4])
        for way, off in ((0, 1), (1, 3)):
            remote(w_cols(zl_now, y), w_cols(zl_now, y), wy_s.at[way, zl_now], wy_r.at[way, zl_now], y_peer(off)).start()

    for o in (2, 6, 4):
        landed(ext.at[:, :, rows_of(0), :], in_r.at[o])
    remote(cot, cot_rows(s), cot_s.at[0], cot_r.at[0], x_peer(1)).start()
    remote(cot, cot_rows(s), cot_s.at[1], cot_r.at[1], x_peer(3)).start()
    for o in (3, 5, 7, 1):
        landed(ext.at[:, :, rows_of(0), :], in_r.at[o])
    landed(ext.at[:, :, rows_of(0), :], in_s.at[0])
    halo = [
        remote(ext.at[1:3, :, 1024:1168, :], ext.at[1:3, :, 0:144, :], halo_s.at[0], halo_r.at[0], block_peer(1)),
        remote(ext.at[0, :, 1152:1168, :], ext.at[0, :, 128:144, :], halo_s.at[1], halo_r.at[1], block_peer(1)),
    ]
    for cp in halo:
        cp.start()
    for i, (src, dst) in enumerate(taps_in):
        landed(dst.at[0], own.at[2 + i])
        landed(dst.at[0], sm_r.at[i])

    started = block > 0
    more = block < 31
    lane = lax.broadcasted_iota(jnp.int32, (16, 128), 1)
    wide = lax.broadcasted_iota(jnp.int32, (128, 128), 1)

    def taps_of(p):
        cols = pl.ds(pl.multiple_of(128 * lax.rem(p, 2), 128), 128)
        return cols, lambda i, j: shorts[p // 2, i, j : j + 1, cols]

    def feature(tap, i, r, rows):
        total = tap(i, 0) * stage[i, pl.ds(r, rows), :]
        for j in range(1, SHORT):
            total = total + tap(i, j) * stage[i, pl.ds(r - j, rows), :]
        return total

    def products(tap, p, b):
        r = HALO + 64 * b
        here = pl.ds(pl.multiple_of(64 * b, 64), 64)
        f0[p, here, :] = feature(tap, 0, r, 64)
        one, two = feature(tap, 1, r, 64), feature(tap, 2, r, 64)
        f1[p, here, :] = one.astype(jnp.bfloat16)
        f2[p, here, :] = two.astype(jnp.bfloat16)
        prod[p, pl.ds(pl.multiple_of(64 * b + 128, 64), 64), :] = one * two

    @pl.loop(0, 4)
    def _(p):
        cols, tap = taps_of(p)

        @pl.loop(0, 8)
        def _(b):
            here = pl.ds(pl.multiple_of(HALO + 128 * b, 16), 128)
            for i in range(3):
                stage[i, here, :] = ext[i, p // 2, here, cols].astype(jnp.float32)

        @pl.loop(1, 16)
        def _(b):
            products(tap, p, b)

    y_left, y_right = lax.rem(y + 3, 4), lax.rem(y + 1, 4)
    for zl_ in range(4):
        landed(w_cols(0, 0), wy_r.at[0, zl_])
        landed(w_cols(0, 0), wy_r.at[1, zl_])
        way, off, col = (0, 1, y_left) if zl_ < 2 else (1, 3, y_right)
        remote(w_cols(zl_, col), w_cols(zl_, col), wy_s.at[2, zl_], wy_r.at[2, zl_], y_peer(off)).start()
    for cp in halo:
        cp.wait_recv()
    s_left, s_right, s_far = lax.rem(s + 6, 8), lax.rem(s + 2, 8), lax.rem(s + 4, 8)

    def grad_in(p):
        rows = pl.ds(pl.multiple_of(256 * lax.rem(x + p + p // 2 - 2 * (p // 3), 4), 256), 256)

        @pl.loop(0, 2)
        def _(n):
            part_w = wg[pl.ds(pl.multiple_of(256 * n, 256), 256), :]
            out = lax.dot_general(cotg[rows, :], part_w, (((1,), (1,)), ((), ())), preferred_element_type=jnp.float32)
            mg[2 * n, rows, :] = out[:, :128]
            mg[2 * n + 1, rows, :] = out[:, 128:]

    @pl.loop(0, 4)
    def _(p):
        slab, half = p // 2, lax.rem(p, 2)
        cols, tap = taps_of(p)
        for i in range(3):
            lead = ext[i, slab, 0:HALO, cols].astype(jnp.float32)
            stage[i, 0:HALO, :] = jnp.where(started, lead, 0.0)
            stage[i, HALO : HALO + 64, :] = ext[i, slab, HALO : HALO + 64, cols].astype(jnp.float32)

        @pl.loop(0, 2)
        def _(b):
            r = HALO - 128 + 64 * b
            prod[p, pl.ds(pl.multiple_of(64 * b, 64), 64), :] = feature(tap, 1, r, 64) * feature(tap, 2, r, 64)

        products(tap, p, 0)

        @pl.loop(0, 8)
        def _(m):
            r = pl.multiple_of(16 * m, 16)
            now = spread([prod[p, pl.ds(128 + 128 * b + r, 16), :] for b in range(8)], lane)
            lead = prod[p, pl.ds(r, 16), :]
            for g in range(8):
                head = lead if g == 0 else pltpu.roll(lead, 128 - 16 * g, 1)
                before = jnp.where(lane < 16, head, pltpu.roll(now[g], 16, 1))
                pgs[8 * p + g, pl.ds(r, 16), :] = before.astype(jnp.bfloat16)
                pgs[8 * p + g, pl.ds(128 + r, 16), :] = now[g].astype(jnp.bfloat16)

        for g in range(8):
            row = tabss[slab, 0, pl.ds(8 * half + g, 1), :]
            table = pltpu.roll(jnp.broadcast_to(row, (128, 256)), 0, 1, stride=1, stride_axis=0)
            group[g] = jnp.dot(table.astype(jnp.bfloat16), pgs[8 * p + g], preferred_element_type=jnp.float32)
        skip = gains[slab, 0:1, cols]

        @pl.loop(0, 8)
        def _(m):
            r = pl.multiple_of(16 * m, 16)
            back = spread([group[g, pl.ds(r, 16), :] for g in range(8)], lane)
            for b in range(8):
                here = pl.ds(pl.multiple_of(128 * b + r, 16), 16)
                whole = back[b] + skip * prod[p, pl.ds(128 * (b + 1) + r, 16), :]
                filt[p, here, :] = whole
                mixed[here, :] = (f0[p, here, :] * whole).astype(jnp.bfloat16)

        for b in range(8):
            turned[pl.ds(pl.multiple_of(128 * p, 128), 128), 128 * b : 128 * b + 128] = mixed[128 * b : 128 * b + 128, :].T

        @pl.when(p == 0)
        def _():
            own_c.wait()
            landed(cot_rows(0), cot_r.at[2])
            for zl_ in range(4):
                landed(w_cols(0, 0), wy_r.at[2, zl_])
            grad_in(0)

        @pl.when(p == 1)
        def _():
            landed(cot_rows(0), cot_r.at[0])
            remote(cot_half(s_left, 0), cot_half(s_left, 0), cot_s.at[3], cot_r.at[3], x_peer(1)).start()
            remote(cot_rows(s_left), cot_rows(s_left), cot_s.at[4], cot_r.at[4], sib).start()
            landed(cot_rows(0), cot_r.at[1])
            remote(cot_half(s_right, 1), cot_half(s_right, 1), cot_s.at[5], cot_r.at[5], x_peer(3)).start()
            remote(cot_rows(s_right), cot_rows(s_right), cot_s.at[6], cot_r.at[6], sib).start()

        @pl.when(p == 2)
        def _():
            landed(cot_rows(0), cot_r.at[4])
            landed(cot_rows(0), cot_r.at[6])

            @pl.loop(1, 3)
            def _(n):
                grad_in(n)

    landed(cot_half(0, 0), cot_r.at[3])
    remote(cot_half(s_far, 0), cot_half(s_far, 0), cot_s.at[7], cot_r.at[7], sib).start()
    landed(cot_half(0, 0), cot_r.at[5])
    remote(cot_half(s_far, 1), cot_half(s_far, 1), cot_s.at[8], cot_r.at[8], sib).start()
    landed(cot_half(0, 0), cot_r.at[7])
    landed(cot_half(0, 0), cot_r.at[8])
    grad_in(3)

    @pl.loop(0, 4)
    def _(p):
        @pl.loop(0, 8)
        def _(m):
            r = pl.multiple_of(16 * m, 16)
            slopes = []
            for b in range(8):
                here = pl.ds(pl.multiple_of(128 * b + r, 16), 16)
                back = mg[p, here, :]
                slope = back * f0[p, here, :]
                qf[p, here, :] = (back * filt[p, here, :]).astype(jnp.bfloat16)
                sl[p, here, :] = slope.astype(jnp.bfloat16)
                slopes.append(slope)
            slopes = spread(slopes, lane)
            for g in range(8):
                dgs[8 * p + g, pl.ds(r, 16), :] = slopes[g].astype(jnp.bfloat16)

        edge_a[p, 0:HALO, :] = sl[p, 0:HALO, :]
        edge_a[p, HALO : HALO + 16, :] = f1[p, 0:16, :]
        edge_a[p, HALO + 16 : HALO + 32, :] = f2[p, 0:16, :]
        edge_a[p, HALO + 32 : HALO + 48, :] = qf[p, 0:16, :]

    edge = remote(edge_a, edge_b, edge_s, edge_r, block_peer(31))
    edge.start()

    @pl.loop(0, 16)
    def _(n):
        o = lax.rem(n + 1, 4)
        to_y = lax.rem(y + o, 4)
        to_zl = lax.rem(zl + n // 4, 4)
        cols = pl.ds(pl.multiple_of(1024 * to_zl + 256 * to_y, 256), 256)
        out = jnp.dot(turned[...], cotg[:, cols], preferred_element_type=jnp.float32).astype(jnp.bfloat16)
        part[to_y, to_zl, 0] = out[:256]
        part[to_y, to_zl, 1] = out[256:]

        @pl.when(o > 0)
        def _():
            for h in range(2):
                kk = lax.rem(4 * h + to_zl - zpos + 8, 8)
                remote(part.at[to_y, to_zl, h], land.at[o - 1, kk], py_s.at[o - 1, kk], py_r.at[o - 1, kk], y_peer(o)).start()

    edge.wait_recv()

    @pl.loop(0, 4)
    def _(p):
        slab, half = p // 2, lax.rem(p, 2)
        cols, tap = taps_of(p)
        for i in range(3):
            lead = ext[i, slab, HALO - 16 : HALO, cols].astype(jnp.float32)
            stage[i, 0:16, :] = jnp.where(started, lead, 0.0)

        @pl.loop(0, 8)
        def _(b):
            for i in range(3):
                rows = ext[i, slab, pl.ds(pl.multiple_of(HALO + 128 * b, 16), 128), cols]
                stage[i, pl.ds(pl.multiple_of(16 + 128 * b, 16), 128), :] = rows.astype(jnp.float32)

        skip = gains[slab, 0:1, cols]
        square = [lax.broadcasted_iota(jnp.int32, (256, 256), a) for a in (0, 1)]
        flip = (square[0] + square[1] == 255).astype(jnp.bfloat16)
        rim = jnp.where(more, edge_b[p].astype(jnp.float32), 0.0)
        after = rim[0:128]
        tail = jnp.concatenate([rim[0:HALO], jnp.zeros((256 - HALO, 128), jnp.float32)], 0).astype(jnp.bfloat16)
        over = jnp.zeros((16, 128), jnp.float32)
        for g in range(8):
            row = tabss[slab, 1, pl.ds(8 * half + g, 1), :]
            table = pltpu.roll(jnp.broadcast_to(row, (128, 256)), 0, 1, stride=1, stride_axis=0).astype(jnp.bfloat16)
            here = dgs[8 * p + g]
            head = after if g == 7 else pltpu.roll(after, 16 * (7 - g), 1)
            later = jnp.where(wide >= 112, head, pltpu.roll(here.astype(jnp.float32), 112, 1)).astype(jnp.bfloat16)
            group[g] = jnp.dot(table, jnp.concatenate([here, later], 0), preferred_element_type=jnp.float32)
            past = jnp.dot(table[:16], tail, preferred_element_type=jnp.float32)
            over = jnp.where(lane // 16 == g, past, over)
            back = jnp.dot(flip, pgs[8 * p + g], preferred_element_type=jnp.float32).astype(jnp.bfloat16)
            gram = lax.dot_general(here, back, (((1,), (1,)), ((), ())), preferred_element_type=jnp.float32)
            lined = pltpu.roll(gram, 0, 1, stride=1, stride_axis=0)
            small[slab, pl.ds(24 + 8 * half + g, 1), :] = jnp.sum(lined, axis=0, keepdims=True)

        def gain_sum(m, total):
            r = pl.multiple_of(16 * m, 16)
            back = spread([group[g, pl.ds(r, 16), :] for g in range(8)], lane)
            for b in range(8):
                here = pl.ds(pl.multiple_of(128 * b + r, 16), 16)
                slope = sl[p, here, :].astype(jnp.float32)
                whole = back[b] + skip * slope
                feat[0, here, :] = qf[p, here, :].astype(jnp.float32)
                feat[1, here, :] = whole * f2[p, here, :].astype(jnp.float32)
                feat[2, here, :] = whole * f1[p, here, :].astype(jnp.float32)
                term = slope * prod[p, pl.ds(128 * (b + 1) + r, 16), :]
                total = total + term[:8] + term[8:]
            return total

        total = lax.fori_loop(0, 8, gain_sum, jnp.zeros((8, 128), jnp.float32))
        over = over + skip * rim[0:16]
        feat[0, 1024:1040, :] = rim[HALO + 32 : HALO + 48]
        feat[1, 1024:1040, :] = over * rim[HALO + 16 : HALO + 32]
        feat[2, 1024:1040, :] = over * rim[HALO : HALO + 16]

        for i in range(3):
            tap_i = [tap(i, j) for j in range(SHORT)]

            def rows_sum(b, sums):
                r = pl.multiple_of(64 * b, 64)
                mine = feat[i, pl.ds(r, 64), :]
                back = tap_i[0] * mine
                for j in range(1, SHORT):
                    back = back + tap_i[j] * feat[i, pl.ds(r + j, 64), :]
                grad[i, slab, pl.ds(r, 64), cols] = back.astype(jnp.bfloat16)
                out = []
                for j in range(SHORT):
                    term = mine * stage[i, pl.ds(16 + r - j, 64), :]
                    out.append(sums[j] + jnp.sum(term.reshape(8, 8, 128), axis=0))
                return tuple(out)

            sums = lax.fori_loop(0, 16, rows_sum, (jnp.zeros((8, 128), jnp.float32),) * SHORT)
            for j in range(SHORT):
                small[slab, 8 * i + j : 8 * i + j + 1, cols] = jnp.sum(sums[j], axis=0, keepdims=True)
            small[slab, 8 * i + SHORT : 8 * i + 8, cols] = jnp.sum(total, axis=0, keepdims=True)

        for o in (2, 6, 3, 5, 4, 7, 1, 0):
            d = lax.rem(s + o, 8)
            to = pl.ds(pl.multiple_of(2048 * slab + 256 * s + 128 * half, 128), 128)
            for i, dst in enumerate((gq, gk, gv)):
                src = grad.at[i, slab, pl.ds(pl.multiple_of(128 * d, 128), 128), cols]
                if o:
                    remote(src, dst.at[:, to], out_s.at[p, o], out_r.at[p, o], group_peer(o)).start()
                else:
                    pltpu.make_async_copy(src, dst.at[:, to], out_s.at[p, 0]).start()

        for m in range(2):
            kk = 2 * p + m
            t = lax.rem(zpos + kk, 8)
            for o in range(3):
                landed(land.at[o, kk], py_r.at[o, kk])

            @pl.loop(0, 4)
            def _(n):
                rows = pl.ds(pl.multiple_of(64 * n, 64), 64)
                total = part[y, lax.rem(t, 4), t // 4, rows, :].astype(jnp.float32)
                for o in range(3):
                    total = total + land[o, kk, rows, :].astype(jnp.float32)
                once[kk, rows, :] = total.astype(jnp.bfloat16)

            @pl.when(kk > 0)
            def _():
                remote(once.at[kk], zland.at[kk], pz_s.at[kk], pz_r.at[kk], z_peer(kk)).start()

    for o in range(1, 4):
        remote(small, small_y.at[o - 1], sy_s.at[o - 1], sy_r.at[o - 1], y_peer(o)).start()
    for kk in range(1, 8):
        landed(zland.at[kk], pz_r.at[kk])

    @pl.loop(0, 4)
    def _(n):
        rows = pl.ds(pl.multiple_of(64 * n, 64), 64)
        total = once[0, rows, :].astype(jnp.float32)
        for kk in range(1, 8):
            total = total + zland[kk, rows, :].astype(jnp.float32)
        wout[rows, :] = total * SCALE

    for o in range(3):
        landed(small, sy_r.at[o])
    small_t[...] = small[...] + small_y[0] + small_y[1] + small_y[2]
    for kk in range(1, 8):
        t = lax.rem(zpos + kk, 8)
        remote(small_t.at[t // 4], small_z.at[kk], sz_s.at[kk], sz_r.at[kk], z_peer(kk)).start()
    for kk in range(1, 8):
        landed(small_z.at[kk], sz_r.at[kk])
    total = small_t[zh]
    for kk in range(1, 8):
        total = total + small_z[kk]
    small_o[...] = total * SCALE

    for i, (src, dst) in enumerate(taps_in):
        landed(dst.at[0], sm_s.at[i])
    for o in range(1, 8):
        landed(w_block(0, 0), wz_s.at[o])
        landed(ext.at[:, :, rows_of(0), :], in_s.at[o])
    for way in range(3):
        for zl_ in range(4):
            landed(w_cols(0, 0), wy_s.at[way, zl_])
    for cp in halo:
        cp.wait_send()
    for n in range(9):
        landed(cot_half(0, 0) if n in (3, 5, 7, 8) else cot_rows(0), cot_s.at[n])
    edge.wait_send()
    for o in range(3):
        landed(small, sy_s.at[o])
        for kk in range(8):
            landed(land.at[o, kk], py_s.at[o, kk])
    for kk in range(1, 8):
        landed(once.at[kk], pz_s.at[kk])
        landed(small_z.at[kk], sz_s.at[kk])
    piece = grad.at[:, 0, 0:128, 0:128]
    for p in range(4):
        for o in range(8):
            landed(piece, out_s.at[p, o])
            if o:
                landed(piece, out_r.at[p, o])


ANY = pl.BlockSpec(memory_space=pl.ANY)


def mixer(q, k, v, cot, w, short, tabs, gain):
    dma = pltpu.SemaphoreType.DMA
    tok = jax.ShapeDtypeStruct((128, 4096), jnp.bfloat16)
    vmem = pl.BlockSpec(memory_space=pltpu.VMEM)
    bf = lambda *shape: pltpu.VMEM(shape, jnp.bfloat16)
    f32 = lambda *shape: pltpu.VMEM(shape, jnp.float32)
    return pl.pallas_call(
        mixer_kernel,
        out_shape=(tok, tok, tok, jax.ShapeDtypeStruct((256, 256), jnp.float32), jax.ShapeDtypeStruct((40, 256), jnp.float32)),
        in_specs=[ANY] * 8,
        out_specs=(ANY,) * 3 + (vmem,) * 2,
        scratch_shapes=[
            bf(3, 2, 1024 + HALO, 256), bf(1024, 4096), bf(512, 4096), f32(2, 3, SHORT, 256), f32(2, 2, 16, 256), f32(2, 1, 256),
            f32(3, 1024 + HALO, 128), f32(3, 1024 + 16, 128), f32(8, 128, 128), f32(4, 1152, 128),
            f32(4, 1024, 128), bf(4, 1024, 128), bf(4, 1024, 128), f32(4, 1024, 128), f32(4, 1024, 128),
            bf(1024, 128), bf(512, 1024), bf(32, 256, 128), bf(32, 128, 128), bf(4, 1024, 128), bf(4, 1024, 128),
            bf(4, HALO + 48, 128), bf(4, HALO + 48, 128), bf(4, 4, 2, 256, 256), bf(3, 2, 1024, 256), f32(2, 40, 256),
            bf(3, 8, 256, 256), bf(8, 256, 256), bf(8, 256, 256),
            f32(3, 2, 40, 256), f32(2, 40, 256), f32(8, 40, 256),
            dma((5,)), dma((3,)), dma((3,)), dma((8,)), dma((8,)), dma((3, 4)), dma((3, 4)), dma((8,)), dma((8,)),
            dma((2,)), dma((2,)), dma((9,)), dma((9,)), dma, dma,
            dma((4, 8)), dma((4, 8)), dma((3, 8)), dma((3, 8)), dma((8,)), dma((8,)),
            dma((3,)), dma((3,)), dma((8,)), dma((8,)),
        ],
        compiler_params=pltpu.CompilerParams(collective_id=0, has_side_effects=True, vmem_limit_bytes=60 * 2**20),
        cost_estimate=pl.CostEstimate(flops=2 * 2 * 512 * 4096 * 1024, bytes_accessed=16 * 2**20, transcendentals=0),
        name="mixer",
    )(q, k, v, cot, w, short, tabs, gain)


def body(q, k, v, cot, w, short_taps, long_taps, skip_gain):
    blank = jnp.zeros((16, 1), jnp.float32)
    turned = long_taps.T
    tables = jnp.stack(
        [
            jnp.concatenate([blank, turned[:, ::-1], jnp.zeros((16, 127), jnp.float32)], 1),
            jnp.concatenate([turned, jnp.zeros((16, 128), jnp.float32)], 1),
        ]
    )
    gq, gk, gv, wout, small = mixer(q, k, v, cot, w, short_taps, tables, skip_gain[None, :])
    return gq, gk, gv, wout, small[:24].reshape(3, 8, 256)[:, :SHORT], small[24:, 127:255].T, small[SHORT]


def solution(mesh):
    fine = Mesh(mesh.devices.reshape(4, 4, 2, 4, 2), AXES)
    tok = P(AXES, None)
    chan = ("zh", "x", "core")
    weight = P(chan, ("zl", "y"))
    small = (P(None, None, chan), P(None, chan), P(chan))
    return jax.shard_map(
        body,
        mesh=fine,
        in_specs=(tok,) * 4 + (weight,) + small,
        out_specs=(tok,) * 3 + (weight,) + small,
        check_vma=False,
    )
```

time: 676 us -> 205 us (0.30)
  waiting for transfers between devices: 255 us -> 0 us
  Pallas kernels: 0 us -> 190 us
  blocking collectives: 163 us -> 0 us
  matrix products: 71.3 us -> 0 us
  local copies, waits for them, and re-layouts: 77.6 us -> 10.7 us
  other arithmetic: 59.4 us -> 0.7 us
  starting transfers between devices: 26.6 us -> 0 us
  between operations: 14.6 us -> 0.66 us
    pallas_call x0 -> x1, Pallas kernels: none -> 190 us  [mixer(): pl.pallas_call(mixer_kernel, out_shape=(tok, tok, tok, jax.ShapeDtypeStru...]
    all_gather x2 -> x0, waiting for transfers between devices: 179 us -> none  [the longest x1 179 us: cotangent_terms(): all_rows = lax.all_gather(cotangent, 'seq', axis=0, tiled=True)]
    psum x1 -> x0, blocking collectives: 163 us -> none  [body(): lax.psum((short_part, long_part, gain_part), 'fsdp')]
    all_to_all x2 -> x0, waiting for transfers between devices: 74 us -> none  [the longest x1 74 us: body(): lax.all_to_all(stacked, 'seq', split_axis=2, concat_axis=1, tiled=True)]
    dot_general x12 -> x0, matrix products: 71.3 us -> none  [the longest x1 16 us: cotangent_terms(): lax.dot_general(all_rows, full_cols, (((1,), (1,)), ((), ())), preferred_...]
    reduce_sum x2 -> x0, other arithmetic: 19.4 us -> none  [short_backward(): jnp.sum(feat_grad * extended[:, begin:begin + row_count], axis=1)]
    unnamed x70 -> x12, local copies, waits for them, and re-layouts: 25 us -> 5.78 us
    all_to_all x2 -> x0, starting transfers between devices: 18.2 us -> none  [the longest x1 11.6 us: body(): lax.all_to_all(stacked, 'seq', split_axis=2, concat_axis=1, tiled=True)]
  transfers between devices with their start and end apart: 9 -> 0, of which waited for: 3 -> 0; matrix products, arithmetic and copies ran while one was open for 24% -> 0% of each run, Pallas kernels for 0% -> 0%
where the time goes in v3:
time: 205 us; the launch traced here: 202 us
  Pallas kernels  190 us (93%)
  local copies, waits for them, and re-layouts  10.7 us (5%)
    pallas_call x1, Pallas kernels, mixer(): pl.pallas_call(mixer_kernel, out_shape=(tok, tok, tok, jax.ShapeDtypeStru...  190 us
    unnamed x12, local copies, waits for them, and re-layouts  5.78 us

profile of v3, /device:TPU:2, one launch (start us, length us, event | category | flops | bytes accessed | tf_op | source)
XLA Modules:
  0.0 201.8 jit_solution(8702820889779289588)
XLA Ops:
  0.6 0.0 copy-start.3
  0.6 0.8 rev.3
  1.5 0.1 pad.5.clone
  1.6 0.0 copy-done.3
  1.6 0.1 maximum_bitcast_fusion
  1.6 0.6 pad_maximum_fusion.tabs
  2.3 189.8 %mixer.1 = (bf16[128,4096]{1,0:T(8,128)(2,1)}, bf16[128,4096]{1,0:T(8,128)(2,1)}, bf16[128,4096]{1,0:T(8,128)(2,1)}, f32[256,256]{1,0:T(8,128)}, f32[40,256]{1,0:T(8,128)}) custom-call(bf16[128,4096]{1,0:T(8,128)(2,1)} %q.1, bf16[128,4096]{1,0:T(8,128)(2,1)} %k.1, bf16[128,4096]{1,0:T(8,128)(2,1)} %v.1, bf16[128,4096]{1,0:T(8,128)(2,1)} %cot.1, ...), custom_call_target="tpu_custom_call" | custom-call | flops 8589934592 | bytes 16777216 | tf_op jit(solution)/shard_map/mixer/pallas_call | solution.py:509
  192.0 1.3 slice_bitcast_fusion
  193.4 1.4 slice_bitcast_fusion.1
  194.8 1.3 slice.15
  196.0 0.0 copy-start.1
  196.0 2.4 %copy.19 = bf16[128,4096]{1,0:T(8,128)(2,1)} copy(bf16[128,4096]{1,0:T(8,128)(2,1)} %get-tuple-element.26) | data formatting | bytes 2097152
  198.4 0.0 copy-done.1
  198.4 0.0 copy-start
  198.4 1.0 copy.20
  199.4 0.6 copy-done
  200.0 0.0 copy-start.2
  200.0 1.0 copy.21
  201.0 0.1 copy-done.2
  201.1 0.7 copy.22
  (2 shorter events, 0.0 us)
Async XLA Ops:
  0.6 0.9 copy-start.3
  196.0 2.4 %copy-start.1 = (bf16[128,4096]{1,0:T(8,128)(2,1)S(1)}, bf16[128,4096]{1,0:T(8,128)(2,1)}, u32[]{:S(2)}) copy-start(bf16[128,4096]{1,0:T(8,128)(2,1)} %get-tuple-element.27) | copy-start | bytes 3145732
  198.4 1.6 copy-start
  200.0 1.1 copy-start.2

commit v4 on v3

--- a/solution.py
+++ b/solution.py
@@ -74,9 +74,9 @@
 
 def mixer_kernel(
     q, k, v, cot, w, short, tabs, gain,
-    gq, gk, gv, wout, small_o,
+    gq, gk, gv, wout, short_o, long_o, gain_o,
     ext, cotg, wg, shorts, tabss, gains,
-    stage, feat, group, prod, f0, f1, f2, filt, mg, mixed, turned, pgs, dgs, sl, qf, edge_a, edge_b, part, grad, small,
+    stage, feat, group, prod, f0, f1, f2, filt, mg, mixed, turned, pgs, dgs, sl, qf, edge_a, edge_b, part, grad, small, held, end, seen,
     land, once, zland, small_y, small_t, small_z,
     own, sm_s, sm_r, wz_s, wz_r, wy_s, wy_r, in_s, in_r, halo_s, halo_r, cot_s, cot_r, edge_s, edge_r,
     out_s, out_r, py_s, py_r, pz_s, pz_r, sy_s, sy_r, sz_s, sz_r,
@@ -232,7 +232,7 @@
 
         products(tap, p, 0)
 
-        @pl.loop(0, 8)
+        @pl.loop(0, 8, unroll=2)
         def _(m):
             r = pl.multiple_of(16 * m, 16)
             now = spread([prod[p, pl.ds(128 + 128 * b + r, 16), :] for b in range(8)], lane)
@@ -249,7 +249,7 @@
             group[g] = jnp.dot(table.astype(jnp.bfloat16), pgs[8 * p + g], preferred_element_type=jnp.float32)
         skip = gains[slab, 0:1, cols]
 
-        @pl.loop(0, 8)
+        @pl.loop(0, 8, unroll=2)
         def _(m):
             r = pl.multiple_of(16 * m, 16)
             back = spread([group[g, pl.ds(r, 16), :] for g in range(8)], lane)
@@ -296,9 +296,8 @@
     landed(cot_half(0, 0), cot_r.at[8])
     grad_in(3)
 
-    @pl.loop(0, 4)
-    def _(p):
-        @pl.loop(0, 8)
+    def gate_grads(p):
+        @pl.loop(0, 8, unroll=2)
         def _(m):
             r = pl.multiple_of(16 * m, 16)
             slopes = []
@@ -318,11 +317,9 @@
         edge_a[p, HALO + 16 : HALO + 32, :] = f2[p, 0:16, :]
         edge_a[p, HALO + 32 : HALO + 48, :] = qf[p, 0:16, :]
 
-    edge = remote(edge_a, edge_b, edge_s, edge_r, block_peer(31))
-    edge.start()
-
-    @pl.loop(0, 16)
-    def _(n):
+        remote(edge_a.at[p], edge_b.at[p], edge_s.at[p], edge_r.at[p], block_peer(31)).start()
+
+    def weight_block(n):
         o = lax.rem(n + 1, 4)
         to_y = lax.rem(y + o, 4)
         to_zl = lax.rem(zl + n // 4, 4)
@@ -337,12 +334,102 @@
                 kk = lax.rem(4 * h + to_zl - zpos + 8, 8)
                 remote(part.at[to_y, to_zl, h], land.at[o - 1, kk], py_s.at[o - 1, kk], py_r.at[o - 1, kk], y_peer(o)).start()
 
-    edge.wait_recv()
+    def sum_along_y(m):
+        for j in range(2):
+            kk = m + 4 * j
+            t = lax.rem(zpos + kk, 8)
+            for o in range(3):
+                landed(land.at[o, kk], py_r.at[o, kk])
+
+            @pl.loop(0, 4)
+            def _(n):
+                rows = pl.ds(pl.multiple_of(64 * n, 64), 64)
+                total = part[y, lax.rem(t, 4), t // 4, rows, :].astype(jnp.float32)
+                for o in range(3):
+                    total = total + land[o, kk, rows, :].astype(jnp.float32)
+                once[kk, rows, :] = total.astype(jnp.bfloat16)
+
+            @pl.when(kk > 0)
+            def _():
+                remote(once.at[kk], zland.at[kk], pz_s.at[kk], pz_r.at[kk], z_peer(kk)).start()
+
+    def skewed(p, g):
+        row = tabss[p // 2, 1, pl.ds(8 * lax.rem(p, 2) + g, 1), :]
+        return pltpu.roll(jnp.broadcast_to(row, (128, 256)), 0, 1, stride=1, stride_axis=0).astype(jnp.bfloat16)
+
+    def send_out(p, low, high):
+        slab, half = p // 2, lax.rem(p, 2)
+        cols = pl.ds(pl.multiple_of(128 * half, 128), 128)
+        to = pl.ds(pl.multiple_of(2048 * slab + 256 * s + 128 * half, 128), 128)
+        for o in (2, 6, 3, 5, 4, 7, 1, 0):
+            d = lax.rem(s + o, 8)
+
+            @pl.when((d >= low) & (d < high))
+            def _():
+                for i, dst in enumerate((gq, gk, gv)):
+                    src = grad.at[i, slab, pl.ds(pl.multiple_of(128 * d, 128), 128), cols]
+                    if o:
+                        remote(src, dst.at[:, to], out_s.at[p, o], out_r.at[p, o], group_peer(o)).start()
+                    else:
+                        pltpu.make_async_copy(src, dst.at[:, to], out_s.at[p, 0]).start()
+
+    def last_rows(p):
+        slab, half = p // 2, lax.rem(p, 2)
+        cols, tap = taps_of(p)
+        skip = gains[slab, 0:1, cols]
+        landed(edge_b.at[p], edge_r.at[p])
+        rim = jnp.where(more, edge_b[p].astype(jnp.float32), 0.0)
+        tail = jnp.concatenate([rim[0:HALO], jnp.zeros((256 - HALO, 128), jnp.float32)], 0).astype(jnp.bfloat16)
+        run = lax.broadcasted_iota(jnp.int32, (HALO, 128), 1) // 16
+        late = jnp.zeros((HALO, 128), jnp.float32)
+        for g in range(8):
+            table = skewed(p, g)
+            left = jnp.concatenate([jnp.concatenate([table[:, 128:], jnp.zeros((128, 128), jnp.bfloat16)], 1), table[:16]], 0)
+            late = jnp.where(run == g, jnp.dot(left, tail, preferred_element_type=jnp.float32), late)
+        whole = held[p, 16:HALO, :] + late[:128]
+        over = late[128:] + skip * rim[0:16]
+        end[0, 0:144, :] = qf[p, 880:1024, :].astype(jnp.float32)
+        end[0, 144:160, :] = rim[HALO + 32 : HALO + 48]
+        for i, other, at in ((1, f2, HALO + 16), (2, f1, HALO)):
+            end[i, 0:16, :] = held[p, 0:16, :] * other[p, 880:896, :].astype(jnp.float32)
+            end[i, 16:144, :] = whole * other[p, 896:1024, :].astype(jnp.float32)
+            end[i, 144:160, :] = over * rim[at : at + 16]
+        for i in range(3):
+            seen[i, :, :] = ext[i, slab, HALO + 864 : HALO + 1024, cols].astype(jnp.float32)
+        for i in range(3):
+            mine = end[i, 0:144, :]
+            back = tap(i, 0) * mine
+            for j in range(1, SHORT):
+                back = back + tap(i, j) * end[i, j : j + 144, :]
+            grad[i, slab, 880:1024, cols] = back.astype(jnp.bfloat16)
+            for j in range(SHORT):
+                row = jnp.sum(mine * seen[i, 16 - j : 160 - j, :], axis=0, keepdims=True)
+                small[p, 8 * i + j : 8 * i + j + 1, :] = small[p, 8 * i + j : 8 * i + j + 1, :] + row
+        send_out(p, 6, 8)
+        for o in range(1, 4):
+            remote(small.at[p], small_y.at[o - 1, p], sy_s.at[o - 1, p], sy_r.at[o - 1, p], y_peer(o)).start()
+
+    def small_along_y(p):
+        for o in range(3):
+            landed(small.at[p], sy_r.at[o, p])
+        small_t[p] = small[p] + small_y[0, p] + small_y[1, p] + small_y[2, p]
+        for kk in range(1, 8):
+            t = lax.rem(zpos + kk, 8)
+
+            @pl.when(t // 4 == p // 2)
+            def _():
+                remote(small_t.at[p], small_z.at[lax.rem(p, 2), kk], sz_s.at[p, kk], sz_r.at[lax.rem(p, 2), kk], z_peer(kk)).start()
 
     @pl.loop(0, 4)
     def _(p):
         slab, half = p // 2, lax.rem(p, 2)
         cols, tap = taps_of(p)
+
+        @pl.loop(0, 4)
+        def _(n):
+            weight_block(4 * p + n)
+
+        gate_grads(p)
         for i in range(3):
             lead = ext[i, slab, HALO - 16 : HALO, cols].astype(jnp.float32)
             stage[i, 0:16, :] = jnp.where(started, lead, 0.0)
@@ -356,23 +443,15 @@
         skip = gains[slab, 0:1, cols]
         square = [lax.broadcasted_iota(jnp.int32, (256, 256), a) for a in (0, 1)]
         flip = (square[0] + square[1] == 255).astype(jnp.bfloat16)
-        rim = jnp.where(more, edge_b[p].astype(jnp.float32), 0.0)
-        after = rim[0:128]
-        tail = jnp.concatenate([rim[0:HALO], jnp.zeros((256 - HALO, 128), jnp.float32)], 0).astype(jnp.bfloat16)
-        over = jnp.zeros((16, 128), jnp.float32)
         for g in range(8):
-            row = tabss[slab, 1, pl.ds(8 * half + g, 1), :]
-            table = pltpu.roll(jnp.broadcast_to(row, (128, 256)), 0, 1, stride=1, stride_axis=0).astype(jnp.bfloat16)
+            table = skewed(p, g)
             here = dgs[8 * p + g]
-            head = after if g == 7 else pltpu.roll(after, 16 * (7 - g), 1)
-            later = jnp.where(wide >= 112, head, pltpu.roll(here.astype(jnp.float32), 112, 1)).astype(jnp.bfloat16)
+            later = jnp.where(wide >= 112, 0.0, pltpu.roll(here.astype(jnp.float32), 112, 1)).astype(jnp.bfloat16)
             group[g] = jnp.dot(table, jnp.concatenate([here, later], 0), preferred_element_type=jnp.float32)
-            past = jnp.dot(table[:16], tail, preferred_element_type=jnp.float32)
-            over = jnp.where(lane // 16 == g, past, over)
             back = jnp.dot(flip, pgs[8 * p + g], preferred_element_type=jnp.float32).astype(jnp.bfloat16)
             gram = lax.dot_general(here, back, (((1,), (1,)), ((), ())), preferred_element_type=jnp.float32)
             lined = pltpu.roll(gram, 0, 1, stride=1, stride_axis=0)
-            small[slab, pl.ds(24 + 8 * half + g, 1), :] = jnp.sum(lined, axis=0, keepdims=True)
+            small[p, 24 + g : 25 + g, :] = pltpu.roll(jnp.sum(lined, axis=0, keepdims=True), 129, 1)[:, :128]
 
         def gain_sum(m, total):
             r = pl.multiple_of(16 * m, 16)
@@ -381,6 +460,10 @@
                 here = pl.ds(pl.multiple_of(128 * b + r, 16), 16)
                 slope = sl[p, here, :].astype(jnp.float32)
                 whole = back[b] + skip * slope
+                if b == 7:
+                    held[p, pl.ds(16 + r, 16), :] = whole
+                if b == 6:
+                    held[p, 0:16, :] = whole
                 feat[0, here, :] = qf[p, here, :].astype(jnp.float32)
                 feat[1, here, :] = whole * f2[p, here, :].astype(jnp.float32)
                 feat[2, here, :] = whole * f1[p, here, :].astype(jnp.float32)
@@ -388,63 +471,45 @@
                 total = total + term[:8] + term[8:]
             return total
 
-        total = lax.fori_loop(0, 8, gain_sum, jnp.zeros((8, 128), jnp.float32))
-        over = over + skip * rim[0:16]
-        feat[0, 1024:1040, :] = rim[HALO + 32 : HALO + 48]
-        feat[1, 1024:1040, :] = over * rim[HALO + 16 : HALO + 32]
-        feat[2, 1024:1040, :] = over * rim[HALO : HALO + 16]
+        total = lax.fori_loop(0, 8, gain_sum, jnp.zeros((8, 128), jnp.float32), unroll=2)
 
         for i in range(3):
             tap_i = [tap(i, j) for j in range(SHORT)]
 
             def rows_sum(b, sums):
-                r = pl.multiple_of(64 * b, 64)
-                mine = feat[i, pl.ds(r, 64), :]
+                r = pl.multiple_of(80 * b, 16)
+                mine = feat[i, pl.ds(r, 80), :]
                 back = tap_i[0] * mine
                 for j in range(1, SHORT):
-                    back = back + tap_i[j] * feat[i, pl.ds(r + j, 64), :]
-                grad[i, slab, pl.ds(r, 64), cols] = back.astype(jnp.bfloat16)
+                    back = back + tap_i[j] * feat[i, pl.ds(r + j, 80), :]
+                grad[i, slab, pl.ds(r, 80), cols] = back.astype(jnp.bfloat16)
                 out = []
                 for j in range(SHORT):
-                    term = mine * stage[i, pl.ds(16 + r - j, 64), :]
-                    out.append(sums[j] + jnp.sum(term.reshape(8, 8, 128), axis=0))
+                    term = mine * stage[i, pl.ds(16 + r - j, 80), :]
+                    out.append(sums[j] + jnp.sum(term.reshape(10, 8, 128), axis=0))
                 return tuple(out)
 
-            sums = lax.fori_loop(0, 16, rows_sum, (jnp.zeros((8, 128), jnp.float32),) * SHORT)
+            sums = lax.fori_loop(0, 11, rows_sum, (jnp.zeros((8, 128), jnp.float32),) * SHORT)
             for j in range(SHORT):
-                small[slab, 8 * i + j : 8 * i + j + 1, cols] = jnp.sum(sums[j], axis=0, keepdims=True)
-            small[slab, 8 * i + SHORT : 8 * i + 8, cols] = jnp.sum(total, axis=0, keepdims=True)
-
-        for o in (2, 6, 3, 5, 4, 7, 1, 0):
-            d = lax.rem(s + o, 8)
-            to = pl.ds(pl.multiple_of(2048 * slab + 256 * s + 128 * half, 128), 128)
-            for i, dst in enumerate((gq, gk, gv)):
-                src = grad.at[i, slab, pl.ds(pl.multiple_of(128 * d, 128), 128), cols]
-                if o:
-                    remote(src, dst.at[:, to], out_s.at[p, o], out_r.at[p, o], group_peer(o)).start()
-                else:
-                    pltpu.make_async_copy(src, dst.at[:, to], out_s.at[p, 0]).start()
-
-        for m in range(2):
-            kk = 2 * p + m
-            t = lax.rem(zpos + kk, 8)
-            for o in range(3):
-                landed(land.at[o, kk], py_r.at[o, kk])
-
-            @pl.loop(0, 4)
-            def _(n):
-                rows = pl.ds(pl.multiple_of(64 * n, 64), 64)
-                total = part[y, lax.rem(t, 4), t // 4, rows, :].astype(jnp.float32)
-                for o in range(3):
-                    total = total + land[o, kk, rows, :].astype(jnp.float32)
-                once[kk, rows, :] = total.astype(jnp.bfloat16)
-
-            @pl.when(kk > 0)
-            def _():
-                remote(once.at[kk], zland.at[kk], pz_s.at[kk], pz_r.at[kk], z_peer(kk)).start()
-
-    for o in range(1, 4):
-        remote(small, small_y.at[o - 1], sy_s.at[o - 1], sy_r.at[o - 1], y_peer(o)).start()
+                small[p, 8 * i + j : 8 * i + j + 1, :] = jnp.sum(sums[j], axis=0, keepdims=True)
+            small[p, 8 * i + SHORT : 8 * i + 8, :] = jnp.sum(total, axis=0, keepdims=True)
+
+        send_out(p, 0, 6)
+
+        @pl.when(p > 0)
+        def _():
+            last_rows(p - 1)
+
+        @pl.when(p > 1)
+        def _():
+            small_along_y(p - 2)
+            sum_along_y(p - 2)
+
+    last_rows(3)
+    small_along_y(2)
+    sum_along_y(2)
+    small_along_y(3)
+    sum_along_y(3)
     for kk in range(1, 8):
         landed(zland.at[kk], pz_r.at[kk])
 
@@ -456,18 +521,16 @@
             total = total + zland[kk, rows, :].astype(jnp.float32)
         wout[rows, :] = total * SCALE
 
-    for o in range(3):
-        landed(small, sy_r.at[o])
-    small_t[...] = small[...] + small_y[0] + small_y[1] + small_y[2]
-    for kk in range(1, 8):
-        t = lax.rem(zpos + kk, 8)
-        remote(small_t.at[t // 4], small_z.at[kk], sz_s.at[kk], sz_r.at[kk], z_peer(kk)).start()
-    for kk in range(1, 8):
-        landed(small_z.at[kk], sz_r.at[kk])
-    total = small_t[zh]
-    for kk in range(1, 8):
-        total = total + small_z[kk]
-    small_o[...] = total * SCALE
+    for half in range(2):
+        total = small_t[2 * zh + half]
+        for kk in range(1, 8):
+            landed(small_z.at[half, kk], sz_r.at[half, kk])
+            total = total + small_z[half, kk]
+        total = total * SCALE
+        for i in range(3):
+            short_o[i, :, 128 * half : 128 * half + 128] = total[8 * i : 8 * i + SHORT]
+        gain_o[:, 128 * half : 128 * half + 128] = total[SHORT : SHORT + 1]
+        long_o[8 * half : 8 * half + 8, :] = total[24:]
 
     for i, (src, dst) in enumerate(taps_in):
         landed(dst.at[0], sm_s.at[i])
@@ -481,14 +544,21 @@
         cp.wait_send()
     for n in range(9):
         landed(cot_half(0, 0) if n in (3, 5, 7, 8) else cot_rows(0), cot_s.at[n])
-    edge.wait_send()
+    for p in range(4):
+        landed(edge_a.at[p], edge_s.at[p])
     for o in range(3):
-        landed(small, sy_s.at[o])
+        for p in range(4):
+            landed(small.at[p], sy_s.at[o, p])
         for kk in range(8):
             landed(land.at[o, kk], py_s.at[o, kk])
     for kk in range(1, 8):
         landed(once.at[kk], pz_s.at[kk])
-        landed(small_z.at[kk], sz_s.at[kk])
+        for p in range(4):
+
+            @pl.when(lax.rem(zpos + kk, 8) // 4 == p // 2)
+            def _():
+                landed(small_t.at[p], sz_s.at[p, kk])
+
     piece = grad.at[:, 0, 0:128, 0:128]
     for p in range(4):
         for o in range(8):
@@ -503,26 +573,27 @@
 def mixer(q, k, v, cot, w, short, tabs, gain):
     dma = pltpu.SemaphoreType.DMA
     tok = jax.ShapeDtypeStruct((128, 4096), jnp.bfloat16)
+    out = lambda *shape: jax.ShapeDtypeStruct(shape, jnp.float32)
     vmem = pl.BlockSpec(memory_space=pltpu.VMEM)
     bf = lambda *shape: pltpu.VMEM(shape, jnp.bfloat16)
     f32 = lambda *shape: pltpu.VMEM(shape, jnp.float32)
     return pl.pallas_call(
         mixer_kernel,
-        out_shape=(tok, tok, tok, jax.ShapeDtypeStruct((256, 256), jnp.float32), jax.ShapeDtypeStruct((40, 256), jnp.float32)),
+        out_shape=(tok, tok, tok, out(256, 256), out(3, SHORT, 256), out(16, 128), out(1, 256)),
         in_specs=[ANY] * 8,
-        out_specs=(ANY,) * 3 + (vmem,) * 2,
+        out_specs=(ANY,) * 3 + (vmem,) * 4,
         scratch_shapes=[
             bf(3, 2, 1024 + HALO, 256), bf(1024, 4096), bf(512, 4096), f32(2, 3, SHORT, 256), f32(2, 2, 16, 256), f32(2, 1, 256),
             f32(3, 1024 + HALO, 128), f32(3, 1024 + 16, 128), f32(8, 128, 128), f32(4, 1152, 128),
             f32(4, 1024, 128), bf(4, 1024, 128), bf(4, 1024, 128), f32(4, 1024, 128), f32(4, 1024, 128),
             bf(1024, 128), bf(512, 1024), bf(32, 256, 128), bf(32, 128, 128), bf(4, 1024, 128), bf(4, 1024, 128),
-            bf(4, HALO + 48, 128), bf(4, HALO + 48, 128), bf(4, 4, 2, 256, 256), bf(3, 2, 1024, 256), f32(2, 40, 256),
+            bf(4, HALO + 48, 128), bf(4, HALO + 48, 128), bf(4, 4, 2, 256, 256), bf(3, 2, 1024, 256), f32(4, 32, 128), f32(4, HALO, 128), f32(3, 160, 128), f32(3, 160, 128),
             bf(3, 8, 256, 256), bf(8, 256, 256), bf(8, 256, 256),
-            f32(3, 2, 40, 256), f32(2, 40, 256), f32(8, 40, 256),
+            f32(3, 4, 32, 128), f32(4, 32, 128), f32(2, 8, 32, 128),
             dma((5,)), dma((3,)), dma((3,)), dma((8,)), dma((8,)), dma((3, 4)), dma((3, 4)), dma((8,)), dma((8,)),
-            dma((2,)), dma((2,)), dma((9,)), dma((9,)), dma, dma,
+            dma((2,)), dma((2,)), dma((9,)), dma((9,)), dma((4,)), dma((4,)),
             dma((4, 8)), dma((4, 8)), dma((3, 8)), dma((3, 8)), dma((8,)), dma((8,)),
-            dma((3,)), dma((3,)), dma((8,)), dma((8,)),
+            dma((3, 4)), dma((3, 4)), dma((4, 8)), dma((2, 8)),
         ],
         compiler_params=pltpu.CompilerParams(collective_id=0, has_side_effects=True, vmem_limit_bytes=60 * 2**20),
         cost_estimate=pl.CostEstimate(flops=2 * 2 * 512 * 4096 * 1024, bytes_accessed=16 * 2**20, transcendentals=0),
@@ -539,8 +610,8 @@
             jnp.concatenate([turned, jnp.zeros((16, 128), jnp.float32)], 1),
         ]
     )
-    gq, gk, gv, wout, small = mixer(q, k, v, cot, w, short_taps, tables, skip_gain[None, :])
-    return gq, gk, gv, wout, small[:24].reshape(3, 8, 256)[:, :SHORT], small[24:, 127:255].T, small[SHORT]
+    gq, gk, gv, wout, short, long, gain = mixer(q, k, v, cot, w, short_taps, tables, skip_gain[None, :])
+    return gq, gk, gv, wout, short, long.T, gain[0]
 
 
 def solution(mesh):

time: 205 us -> 177 us (0.86)
  Pallas kernels: 190 us -> 164 us
  local copies, waits for them, and re-layouts: 10.7 us -> 8.48 us
    pallas_call x1, Pallas kernels: 190 us -> 164 us  [mixer(): pl.pallas_call(mixer_kernel, out_shape=(tok, tok, tok, out(256, 256), out...]
    unnamed x12 -> x21, local copies, waits for them, and re-layouts: 5.78 us -> 8.33 us
where the time goes in v4:
time: 177 us; the launch traced here: 174 us
  Pallas kernels  164 us (93%)
  local copies, waits for them, and re-layouts  8.48 us (5%)
    pallas_call x1, Pallas kernels, mixer(): pl.pallas_call(mixer_kernel, out_shape=(tok, tok, tok, out(256, 256), out...  164 us
    unnamed x21, local copies, waits for them, and re-layouts  8.33 us

profile of v4, /device:TPU:2, one launch (start us, length us, event | category | flops | bytes accessed | tf_op | source)
XLA Modules:
  0.0 174.0 jit_solution(18466296866937157)
XLA Ops:
  0.6 0.0 copy-start.3
  0.7 0.1 pad.5.clone
  0.7 0.6 copy-done.3
  1.3 0.1 rev.3
  1.4 0.1 maximum_bitcast_fusion
  1.5 0.6 pad_maximum_fusion.tabs
  2.1 164.1 %mixer.1 = (bf16[128,4096]{1,0:T(8,128)(2,1)}, bf16[128,4096]{1,0:T(8,128)(2,1)}, bf16[128,4096]{1,0:T(8,128)(2,1)}, f32[256,256]{1,0:T(8,128)}, f32[3,7,256]{2,...) custom-call(bf16[128,4096]{1,0:T(8,128)(2,1)} %q.1, bf16[128,4096]{1,0:T(8,128)(2,1)} %k.1, bf16[128,4096]{1,0:T(8,128)(2,1)} %v.1, ...), custom_call_target="tpu_custom_call" | custom-call | flops 8589934592 | bytes 16777216 | tf_op jit(solution)/shard_map/mixer/pallas_call | solution.py:580
  166.2 0.0 copy-start.1
  166.3 2.4 %copy.22 = bf16[128,4096]{1,0:T(8,128)(2,1)} copy(bf16[128,4096]{1,0:T(8,128)(2,1)} %get-tuple-element.30) | data formatting | bytes 2097152
  168.6 0.0 copy-done.1
  168.6 0.0 copy-start
  168.6 1.0 copy.23
  169.6 0.6 copy-done
  170.2 0.0 copy-start.2
  170.2 1.0 copy.24
  171.2 0.1 copy-done.2
  171.3 0.0 copy-start.4
  171.3 0.7 copy.25
  172.0 0.0 copy-done.4
  172.1 0.0 copy-start.5
  172.1 0.6 copy.26
  172.7 0.1 copy-done.5
  172.8 0.0 copy-start.6
  172.8 0.6 copy.27
  173.4 0.1 copy-done.6
  173.4 0.6 copy.28
  (2 shorter events, 0.0 us)
Async XLA Ops:
  0.6 0.7 copy-start.3
  166.2 2.4 %copy-start.1 = (bf16[128,4096]{1,0:T(8,128)(2,1)S(1)}, bf16[128,4096]{1,0:T(8,128)(2,1)}, u32[]{:S(2)}) copy-start(bf16[128,4096]{1,0:T(8,128)(2,1)} %get-tuple-element.31) | copy-start | bytes 3145732
  168.6 1.6 copy-start
  170.2 1.1 copy-start.2
  171.3 0.7 copy-start.4
  172.1 0.7 copy-start.5
  172.8 0.7 copy-start.6

commit v5 on v4

--- a/solution.py
+++ b/solution.py
@@ -77,7 +77,7 @@
     gq, gk, gv, wout, short_o, long_o, gain_o,
     ext, cotg, wg, shorts, tabss, gains,
     stage, feat, group, prod, f0, f1, f2, filt, mg, mixed, turned, pgs, dgs, sl, qf, edge_a, edge_b, part, grad, small, held, end, seen,
-    land, once, zland, small_y, small_t, small_z,
+    land, joint, once, zland, small_y, small_t, small_z,
     own, sm_s, sm_r, wz_s, wz_r, wy_s, wy_r, in_s, in_r, halo_s, halo_r, cot_s, cot_r, edge_s, edge_r,
     out_s, out_r, py_s, py_r, pz_s, pz_r, sy_s, sy_r, sz_s, sz_r,
 ):
@@ -320,7 +320,7 @@
         remote(edge_a.at[p], edge_b.at[p], edge_s.at[p], edge_r.at[p], block_peer(31)).start()
 
     def weight_block(n):
-        o = lax.rem(n + 1, 4)
+        o = lax.rem(2 + 3 * lax.rem(n, 4), 4)
         to_y = lax.rem(y + o, 4)
         to_zl = lax.rem(zl + n // 4, 4)
         cols = pl.ds(pl.multiple_of(1024 * to_zl + 256 * to_y, 256), 256)
@@ -328,25 +328,45 @@
         part[to_y, to_zl, 0] = out[:256]
         part[to_y, to_zl, 1] = out[256:]
 
-        @pl.when(o > 0)
-        def _():
-            for h in range(2):
-                kk = lax.rem(4 * h + to_zl - zpos + 8, 8)
-                remote(part.at[to_y, to_zl, h], land.at[o - 1, kk], py_s.at[o - 1, kk], py_r.at[o - 1, kk], y_peer(o)).start()
+        for h in range(2):
+            kk = lax.rem(4 * h + to_zl - zpos + 8, 8)
+            mine = part.at[to_y, to_zl, h]
+
+            def send(kind, peer):
+                remote(mine, land.at[kind, kk], py_s.at[kind, kk], py_r.at[kind, kk], peer).start()
+
+            pl.when((o == 2) & (kk < 4))(lambda: send(1, y_peer(1)))
+            pl.when((o == 2) & (kk >= 4))(lambda: send(1, y_peer(3)))
+            pl.when((o == 1) & (kk >= 4))(lambda: send(0, y_peer(1)))
+            pl.when((o == 3) & (kk < 4))(lambda: send(0, y_peer(3)))
+
+    def pass_on(m):
+        for j, off in ((0, 1), (1, 3)):
+            kk = m + 4 * j
+            t = lax.rem(zpos + kk, 8)
+            landed(land.at[1, kk], py_r.at[1, kk])
+
+            @pl.loop(0, 4)
+            def _(n):
+                rows = pl.ds(pl.multiple_of(64 * n, 64), 64)
+                total = part[lax.rem(y + off, 4), lax.rem(t, 4), t // 4, rows, :].astype(jnp.float32)
+                joint[kk, rows, :] = (total + land[1, kk, rows, :].astype(jnp.float32)).astype(jnp.bfloat16)
+
+            remote(joint.at[kk], land.at[2, kk], py_s.at[2, kk], py_r.at[2, kk], y_peer(off)).start()
 
     def sum_along_y(m):
         for j in range(2):
             kk = m + 4 * j
             t = lax.rem(zpos + kk, 8)
-            for o in range(3):
-                landed(land.at[o, kk], py_r.at[o, kk])
+            for kind in (0, 2):
+                landed(land.at[kind, kk], py_r.at[kind, kk])
 
             @pl.loop(0, 4)
             def _(n):
                 rows = pl.ds(pl.multiple_of(64 * n, 64), 64)
                 total = part[y, lax.rem(t, 4), t // 4, rows, :].astype(jnp.float32)
-                for o in range(3):
-                    total = total + land[o, kk, rows, :].astype(jnp.float32)
+                for kind in (0, 2):
+                    total = total + land[kind, kk, rows, :].astype(jnp.float32)
                 once[kk, rows, :] = total.astype(jnp.bfloat16)
 
             @pl.when(kk > 0)
@@ -495,21 +515,21 @@
             small[p, 8 * i + SHORT : 8 * i + 8, :] = jnp.sum(total, axis=0, keepdims=True)
 
         send_out(p, 0, 6)
+        pass_on(p)
 
         @pl.when(p > 0)
         def _():
             last_rows(p - 1)
+            sum_along_y(p - 1)
 
         @pl.when(p > 1)
         def _():
             small_along_y(p - 2)
-            sum_along_y(p - 2)
 
     last_rows(3)
     small_along_y(2)
-    sum_along_y(2)
+    sum_along_y(3)
     small_along_y(3)
-    sum_along_y(3)
     for kk in range(1, 8):
         landed(zland.at[kk], pz_r.at[kk])
 
@@ -588,7 +608,7 @@
             f32(4, 1024, 128), bf(4, 1024, 128), bf(4, 1024, 128), f32(4, 1024, 128), f32(4, 1024, 128),
             bf(1024, 128), bf(512, 1024), bf(32, 256, 128), bf(32, 128, 128), bf(4, 1024, 128), bf(4, 1024, 128),
             bf(4, HALO + 48, 128), bf(4, HALO + 48, 128), bf(4, 4, 2, 256, 256), bf(3, 2, 1024, 256), f32(4, 32, 128), f32(4, HALO, 128), f32(3, 160, 128), f32(3, 160, 128),
-            bf(3, 8, 256, 256), bf(8, 256, 256), bf(8, 256, 256),
+            bf(3, 8, 256, 256), bf(8, 256, 256), bf(8, 256, 256), bf(8, 256, 256),
             f32(3, 4, 32, 128), f32(4, 32, 128), f32(2, 8, 32, 128),
             dma((5,)), dma((3,)), dma((3,)), dma((8,)), dma((8,)), dma((3, 4)), dma((3, 4)), dma((8,)), dma((8,)),
             dma((2,)), dma((2,)), dma((9,)), dma((9,)), dma((4,)), dma((4,)),

time: 177 us -> 163 us (0.921)
  the two profiles are of different devices: /device:TPU:2 before, /device:TPU:207 now
where the time goes in v5:
time: 163 us
  Pallas kernels  153 us (94%)
  local copies, waits for them, and re-layouts  8.48 us (5%)
    pallas_call x1, Pallas kernels, mixer(): pl.pallas_call(mixer_kernel, out_shape=(tok, tok, tok, out(256, 256), out...  153 us
    unnamed x21, local copies, waits for them, and re-layouts  8.33 us

profile of v5, /device:TPU:207, one launch (start us, length us, event | category | flops | bytes accessed | tf_op | source)
XLA Modules:
  0.0 162.8 jit_solution(18343285345192918577)
XLA Ops:
  0.6 0.0 copy-start.3
  0.7 0.1 pad.5.clone
  0.7 0.6 copy-done.3
  1.3 0.1 rev.3
  1.4 0.1 maximum_bitcast_fusion
  1.5 0.6 pad_maximum_fusion.tabs
  2.1 153.0 %mixer.1 = (bf16[128,4096]{1,0:T(8,128)(2,1)}, bf16[128,4096]{1,0:T(8,128)(2,1)}, bf16[128,4096]{1,0:T(8,128)(2,1)}, f32[256,256]{1,0:T(8,128)}, f32[3,7,256]{2,...) custom-call(bf16[128,4096]{1,0:T(8,128)(2,1)} %q.1, bf16[128,4096]{1,0:T(8,128)(2,1)} %k.1, bf16[128,4096]{1,0:T(8,128)(2,1)} %v.1, ...), custom_call_target="tpu_custom_call" | custom-call | flops 8589934592 | bytes 16777216 | tf_op jit(solution)/shard_map/mixer/pallas_call | solution.py:600
  155.1 0.0 copy-start.1
  155.1 2.4 %copy.22 = bf16[128,4096]{1,0:T(8,128)(2,1)} copy(bf16[128,4096]{1,0:T(8,128)(2,1)} %get-tuple-element.30) | data formatting | bytes 2097152
  157.5 0.0 copy-done.1
  157.5 0.0 copy-start
  157.5 1.0 copy.23
  158.4 0.6 copy-done
  159.1 0.0 copy-start.2
  159.1 1.0 copy.24
  160.0 0.1 copy-done.2
  160.2 0.0 copy-start.4
  160.2 0.7 copy.25
  160.9 0.0 copy-done.4
  160.9 0.0 copy-start.5
  160.9 0.6 copy.26
  161.5 0.1 copy-done.5
  161.6 0.0 copy-start.6
  161.6 0.6 copy.27
  162.2 0.1 copy-done.6
  162.3 0.6 copy.28
  (2 shorter events, 0.0 us)
Async XLA Ops:
  0.6 0.7 copy-start.3
  155.1 2.4 %copy-start.1 = (bf16[128,4096]{1,0:T(8,128)(2,1)S(1)}, bf16[128,4096]{1,0:T(8,128)(2,1)}, u32[]{:S(2)}) copy-start(bf16[128,4096]{1,0:T(8,128)(2,1)} %get-tuple-element.31) | copy-start | bytes 3145732
  157.5 1.6 copy-start
  159.1 1.1 copy-start.2
  160.2 0.7 copy-start.4
  160.9 0.7 copy-start.5
  161.6 0.7 copy-start.6

commit v6 on v5

--- a/solution.py
+++ b/solution.py
@@ -10,6 +10,7 @@
 HALO = 144
 SHORT = 7
 SCALE = 32768.0 ** -0.5
+NEAR = (0, 1, 7, 2, 6, 3, 5, 4)
 AXES = ("zl", "y", "zh", "x", "core")
 
 
@@ -106,12 +107,13 @@
     def w_block(zh_, f_):
         return wg.at[pl.ds(pl.multiple_of(256 * zh_, 256), 256), pl.ds(pl.multiple_of(256 * f_, 256), 256)]
 
-    def w_cols(zl_, y_):
-        return wg.at[:, pl.ds(pl.multiple_of(1024 * zl_ + 256 * y_, 256), 256)]
+    def w_from(k, y_):
+        at = lax.rem(zpos + 8 - k, 8)
+        return w_block(at // 4, 4 * lax.rem(at, 4) + y_)
 
     own_w = pltpu.make_async_copy(w, w_block(zh, f), own.at[0])
     own_w.start()
-    for o in range(1, 8):
+    for o in NEAR[1:]:
         remote(w, w_block(zh, f), wz_s.at[o], wz_r.at[o], z_peer(o)).start()
     for o in (2, 6, 4, 3, 5, 7, 1, 0):
         d = lax.rem(s + o, 8)
@@ -132,19 +134,22 @@
     remote(cot, cot_rows(s), cot_s.at[2], cot_r.at[2], sib).start()
 
     own_w.wait()
-    landed(w_block(0, 0), wz_r.at[4])
-    for zl_ in range(4):
-        zl_now = lax.rem(zl + 4 - zl_, 4)
-        if zl_:
-            landed(w_block(0, 0), wz_r.at[zl_])
-            landed(w_block(0, 0), wz_r.at[zl_ + 4])
+    for k in NEAR:
+        if k:
+            landed(w_block(0, 0), wz_r.at[k])
         for way, off in ((0, 1), (1, 3)):
-            remote(w_cols(zl_now, y), w_cols(zl_now, y), wy_s.at[way, zl_now], wy_r.at[way, zl_now], y_peer(off)).start()
+            remote(w_from(k, y), w_from(k, y), wy_s.at[way, k], wy_r.at[way, k], y_peer(off)).start()
 
     for o in (2, 6, 4):
         landed(ext.at[:, :, rows_of(0), :], in_r.at[o])
-    remote(cot, cot_rows(s), cot_s.at[0], cot_r.at[0], x_peer(1)).start()
-    remote(cot, cot_rows(s), cot_s.at[1], cot_r.at[1], x_peer(3)).start()
+    for n, half, off in ((0, 0, 1), (1, 1, 3), (9, 1, 1), (10, 0, 3)):
+        remote(cot.at[64 * half : 64 * half + 64, :], cot_half(s, half), cot_s.at[n], cot_r.at[n], x_peer(off)).start()
+    y_left, y_right = lax.rem(y + 3, 4), lax.rem(y + 1, 4)
+    for n, k in enumerate(NEAR):
+        landed(w_block(0, 0), wy_r.at[0, k])
+        landed(w_block(0, 0), wy_r.at[1, k])
+        off, col = ((1, y_left), (3, y_right))[n % 2]
+        remote(w_from(k, col), w_from(k, col), wy_s.at[2, k], wy_r.at[2, k], y_peer(off)).start()
     for o in (3, 5, 7, 1):
         landed(ext.at[:, :, rows_of(0), :], in_r.at[o])
     landed(ext.at[:, :, rows_of(0), :], in_s.at[0])
@@ -196,15 +201,14 @@
         def _(b):
             products(tap, p, b)
 
-    y_left, y_right = lax.rem(y + 3, 4), lax.rem(y + 1, 4)
-    for zl_ in range(4):
-        landed(w_cols(0, 0), wy_r.at[0, zl_])
-        landed(w_cols(0, 0), wy_r.at[1, zl_])
-        way, off, col = (0, 1, y_left) if zl_ < 2 else (1, 3, y_right)
-        remote(w_cols(zl_, col), w_cols(zl_, col), wy_s.at[2, zl_], wy_r.at[2, zl_], y_peer(off)).start()
+    s_left, s_right, s_far = lax.rem(s + 6, 8), lax.rem(s + 2, 8), lax.rem(s + 4, 8)
+    landed(cot_half(0, 0), cot_r.at[0])
+    remote(cot_half(s_left, 0), cot_half(s_left, 0), cot_s.at[3], cot_r.at[3], x_peer(1)).start()
+    landed(cot_half(0, 0), cot_r.at[1])
+    remote(cot_half(s_right, 1), cot_half(s_right, 1), cot_s.at[5], cot_r.at[5], x_peer(3)).start()
+
     for cp in halo:
         cp.wait_recv()
-    s_left, s_right, s_far = lax.rem(s + 6, 8), lax.rem(s + 2, 8), lax.rem(s + 4, 8)
 
     def grad_in(p):
         rows = pl.ds(pl.multiple_of(256 * lax.rem(x + p + p // 2 - 2 * (p // 3), 4), 256), 256)
@@ -266,27 +270,20 @@
         def _():
             own_c.wait()
             landed(cot_rows(0), cot_r.at[2])
-            for zl_ in range(4):
-                landed(w_cols(0, 0), wy_r.at[2, zl_])
+            for k in range(8):
+                landed(w_block(0, 0), wy_r.at[2, k])
             grad_in(0)
 
-        @pl.when(p == 1)
-        def _():
-            landed(cot_rows(0), cot_r.at[0])
-            remote(cot_half(s_left, 0), cot_half(s_left, 0), cot_s.at[3], cot_r.at[3], x_peer(1)).start()
-            remote(cot_rows(s_left), cot_rows(s_left), cot_s.at[4], cot_r.at[4], sib).start()
-            landed(cot_rows(0), cot_r.at[1])
-            remote(cot_half(s_right, 1), cot_half(s_right, 1), cot_s.at[5], cot_r.at[5], x_peer(3)).start()
-            remote(cot_rows(s_right), cot_rows(s_right), cot_s.at[6], cot_r.at[6], sib).start()
-
-        @pl.when(p == 2)
-        def _():
-            landed(cot_rows(0), cot_r.at[4])
-            landed(cot_rows(0), cot_r.at[6])
-
-            @pl.loop(1, 3)
-            def _(n):
-                grad_in(n)
+    landed(cot_half(0, 0), cot_r.at[9])
+    remote(cot_rows(s_left), cot_rows(s_left), cot_s.at[4], cot_r.at[4], sib).start()
+    landed(cot_half(0, 0), cot_r.at[10])
+    remote(cot_rows(s_right), cot_rows(s_right), cot_s.at[6], cot_r.at[6], sib).start()
+    landed(cot_rows(0), cot_r.at[4])
+    landed(cot_rows(0), cot_r.at[6])
+
+    @pl.loop(1, 3)
+    def _(n):
+        grad_in(n)
 
     landed(cot_half(0, 0), cot_r.at[3])
     remote(cot_half(s_far, 0), cot_half(s_far, 0), cot_s.at[7], cot_r.at[7], sib).start()
@@ -558,12 +555,12 @@
         landed(w_block(0, 0), wz_s.at[o])
         landed(ext.at[:, :, rows_of(0), :], in_s.at[o])
     for way in range(3):
-        for zl_ in range(4):
-            landed(w_cols(0, 0), wy_s.at[way, zl_])
+        for k in range(8):
+            landed(w_block(0, 0), wy_s.at[way, k])
     for cp in halo:
         cp.wait_send()
-    for n in range(9):
-        landed(cot_half(0, 0) if n in (3, 5, 7, 8) else cot_rows(0), cot_s.at[n])
+    for n in range(11):
+        landed(cot_rows(0) if n in (2, 4, 6) else cot_half(0, 0), cot_s.at[n])
     for p in range(4):
         landed(edge_a.at[p], edge_s.at[p])
     for o in range(3):
@@ -610,8 +607,8 @@
             bf(4, HALO + 48, 128), bf(4, HALO + 48, 128), bf(4, 4, 2, 256, 256), bf(3, 2, 1024, 256), f32(4, 32, 128), f32(4, HALO, 128), f32(3, 160, 128), f32(3, 160, 128),
             bf(3, 8, 256, 256), bf(8, 256, 256), bf(8, 256, 256), bf(8, 256, 256),
             f32(3, 4, 32, 128), f32(4, 32, 128), f32(2, 8, 32, 128),
-            dma((5,)), dma((3,)), dma((3,)), dma((8,)), dma((8,)), dma((3, 4)), dma((3, 4)), dma((8,)), dma((8,)),
-            dma((2,)), dma((2,)), dma((9,)), dma((9,)), dma((4,)), dma((4,)),
+            dma((5,)), dma((3,)), dma((3,)), dma((8,)), dma((8,)), dma((3, 8)), dma((3, 8)), dma((8,)), dma((8,)),
+            dma((2,)), dma((2,)), dma((11,)), dma((11,)), dma((4,)), dma((4,)),
             dma((4, 8)), dma((4, 8)), dma((3, 8)), dma((3, 8)), dma((8,)), dma((8,)),
             dma((3, 4)), dma((3, 4)), dma((4, 8)), dma((2, 8)),
         ],

time: 163 us -> 158 us (0.969)
  the two profiles are of different devices: /device:TPU:207 before, /device:TPU:2 now
where the time goes in v6:
time: 158 us; the launch traced here: 156 us
  Pallas kernels  146 us (92%)
  local copies, waits for them, and re-layouts  8.48 us (5%)
    pallas_call x1, Pallas kernels, mixer(): pl.pallas_call(mixer_kernel, out_shape=(tok, tok, tok, out(256, 256), out...  146 us
    unnamed x21, local copies, waits for them, and re-layouts  8.33 us

profile of v6, /device:TPU:2, one launch (start us, length us, event | category | flops | bytes accessed | tf_op | source)
XLA Modules:
  0.0 156.0 jit_solution(5114383369279457266)
XLA Ops:
  0.6 0.0 copy-start.3
  0.7 0.1 pad.5.clone
  0.7 0.6 copy-done.3
  1.3 0.1 rev.3
  1.4 0.1 maximum_bitcast_fusion
  1.5 0.6 pad_maximum_fusion.tabs
  2.1 146.2 %mixer.1 = (bf16[128,4096]{1,0:T(8,128)(2,1)}, bf16[128,4096]{1,0:T(8,128)(2,1)}, bf16[128,4096]{1,0:T(8,128)(2,1)}, f32[256,256]{1,0:T(8,128)}, f32[3,7,256]{2,...) custom-call(bf16[128,4096]{1,0:T(8,128)(2,1)} %q.1, bf16[128,4096]{1,0:T(8,128)(2,1)} %k.1, bf16[128,4096]{1,0:T(8,128)(2,1)} %v.1, ...), custom_call_target="tpu_custom_call" | custom-call | flops 8589934592 | bytes 16777216 | tf_op jit(solution)/shard_map/mixer/pallas_call | solution.py:597
  148.3 0.0 copy-start.1
  148.3 2.4 %copy.22 = bf16[128,4096]{1,0:T(8,128)(2,1)} copy(bf16[128,4096]{1,0:T(8,128)(2,1)} %get-tuple-element.30) | data formatting | bytes 2097152
  150.7 0.0 copy-done.1
  150.7 0.0 copy-start
  150.7 1.0 copy.23
  151.7 0.6 copy-done
  152.3 0.0 copy-start.2
  152.3 1.0 copy.24
  153.3 0.1 copy-done.2
  153.4 0.0 copy-start.4
  153.4 0.7 copy.25
  154.1 0.0 copy-done.4
  154.1 0.0 copy-start.5
  154.1 0.6 copy.26
  154.7 0.1 copy-done.5
  154.8 0.0 copy-start.6
  154.8 0.6 copy.27
  155.4 0.1 copy-done.6
  155.5 0.6 copy.28
  (2 shorter events, 0.0 us)
Async XLA Ops:
  0.6 0.7 copy-start.3
  148.3 2.4 %copy-start.1 = (bf16[128,4096]{1,0:T(8,128)(2,1)S(1)}, bf16[128,4096]{1,0:T(8,128)(2,1)}, u32[]{:S(2)}) copy-start(bf16[128,4096]{1,0:T(8,128)(2,1)} %get-tuple-element.31) | copy-start | bytes 3145732
  150.7 1.6 %copy-start = (bf16[128,4096]{1,0:T(8,128)(2,1)S(1)}, bf16[128,4096]{1,0:T(8,128)(2,1)}, u32[]{:S(2)}) copy-start(bf16[128,4096]{1,0:T(8,128)(2,1)} %get-tuple-element.32) | copy-start | bytes 3145732
  152.3 1.1 copy-start.2
  153.4 0.7 copy-start.4
  154.1 0.7 copy-start.5
  154.8 0.7 copy-start.6

commit v7 on v6

--- a/solution.py
+++ b/solution.py
@@ -140,7 +140,7 @@
         for way, off in ((0, 1), (1, 3)):
             remote(w_from(k, y), w_from(k, y), wy_s.at[way, k], wy_r.at[way, k], y_peer(off)).start()
 
-    for o in (2, 6, 4):
+    for o in (2, 6):
         landed(ext.at[:, :, rows_of(0), :], in_r.at[o])
     for n, half, off in ((0, 0, 1), (1, 1, 3), (9, 1, 1), (10, 0, 3)):
         remote(cot.at[64 * half : 64 * half + 64, :], cot_half(s, half), cot_s.at[n], cot_r.at[n], x_peer(off)).start()
@@ -150,7 +150,7 @@
         landed(w_block(0, 0), wy_r.at[1, k])
         off, col = ((1, y_left), (3, y_right))[n % 2]
         remote(w_from(k, col), w_from(k, col), wy_s.at[2, k], wy_r.at[2, k], y_peer(off)).start()
-    for o in (3, 5, 7, 1):
+    for o in (4, 3, 5, 7, 1):
         landed(ext.at[:, :, rows_of(0), :], in_r.at[o])
     landed(ext.at[:, :, rows_of(0), :], in_s.at[0])
     halo = [
@@ -490,6 +490,7 @@
 
         total = lax.fori_loop(0, 8, gain_sum, jnp.zeros((8, 128), jnp.float32), unroll=2)
 
+        pass_on(p)
         for i in range(3):
             tap_i = [tap(i, j) for j in range(SHORT)]
 
@@ -512,20 +513,19 @@
             small[p, 8 * i + SHORT : 8 * i + 8, :] = jnp.sum(total, axis=0, keepdims=True)
 
         send_out(p, 0, 6)
-        pass_on(p)
 
         @pl.when(p > 0)
         def _():
+            sum_along_y(p - 1)
             last_rows(p - 1)
-            sum_along_y(p - 1)
 
         @pl.when(p > 1)
         def _():
             small_along_y(p - 2)
 
     last_rows(3)
+    sum_along_y(3)
     small_along_y(2)
-    sum_along_y(3)
     small_along_y(3)
     for kk in range(1, 8):
         landed(zland.at[kk], pz_r.at[kk])

time: 158 us -> 159 us (level)
  no operation moved by 1% of the time
where the time goes in v7:
time: 159 us; the launch traced here: 157 us
  Pallas kernels  147 us (92%)
  local copies, waits for them, and re-layouts  8.48 us (5%)
    pallas_call x1, Pallas kernels, mixer(): pl.pallas_call(mixer_kernel, out_shape=(tok, tok, tok, out(256, 256), out...  147 us
    unnamed x21, local copies, waits for them, and re-layouts  8.33 us

profile of v7, /device:TPU:2, one launch (start us, length us, event | category | flops | bytes accessed | tf_op | source)
XLA Modules:
  0.0 156.8 jit_solution(3412417661515745736)
XLA Ops:
  0.6 0.0 copy-start.3
  0.7 0.1 pad.5.clone
  0.7 0.6 copy-done.3
  1.3 0.1 rev.3
  1.4 0.1 maximum_bitcast_fusion
  1.5 0.6 pad_maximum_fusion.tabs
  2.1 146.9 %mixer.1 = (bf16[128,4096]{1,0:T(8,128)(2,1)}, bf16[128,4096]{1,0:T(8,128)(2,1)}, bf16[128,4096]{1,0:T(8,128)(2,1)}, f32[256,256]{1,0:T(8,128)}, f32[3,7,256]{2,...) custom-call(bf16[128,4096]{1,0:T(8,128)(2,1)} %q.1, bf16[128,4096]{1,0:T(8,128)(2,1)} %k.1, bf16[128,4096]{1,0:T(8,128)(2,1)} %v.1, ...), custom_call_target="tpu_custom_call" | custom-call | flops 8589934592 | bytes 16777216 | tf_op jit(solution)/shard_map/mixer/pallas_call | solution.py:597
  149.1 0.0 copy-start.1
  149.1 2.4 %copy.22 = bf16[128,4096]{1,0:T(8,128)(2,1)} copy(bf16[128,4096]{1,0:T(8,128)(2,1)} %get-tuple-element.30) | data formatting | bytes 2097152
  151.4 0.0 copy-done.1
  151.4 0.0 copy-start
  151.4 1.0 copy.23
  152.4 0.6 copy-done
  153.1 0.0 copy-start.2
  153.1 1.0 copy.24
  154.0 0.1 copy-done.2
  154.1 0.0 copy-start.4
  154.1 0.7 copy.25
  154.8 0.0 copy-done.4
  154.9 0.0 copy-start.5
  154.9 0.6 copy.26
  155.5 0.1 copy-done.5
  155.6 0.0 copy-start.6
  155.6 0.6 copy.27
  156.2 0.1 copy-done.6
  156.2 0.6 copy.28
  (2 shorter events, 0.0 us)
Async XLA Ops:
  0.6 0.7 copy-start.3
  149.1 2.4 %copy-start.1 = (bf16[128,4096]{1,0:T(8,128)(2,1)S(1)}, bf16[128,4096]{1,0:T(8,128)(2,1)}, u32[]{:S(2)}) copy-start(bf16[128,4096]{1,0:T(8,128)(2,1)} %get-tuple-element.31) | copy-start | bytes 3145732
  151.4 1.6 %copy-start = (bf16[128,4096]{1,0:T(8,128)(2,1)S(1)}, bf16[128,4096]{1,0:T(8,128)(2,1)}, u32[]{:S(2)}) copy-start(bf16[128,4096]{1,0:T(8,128)(2,1)} %get-tuple-element.32) | copy-start | bytes 3145732
  153.1 1.1 copy-start.2
  154.1 0.7 copy-start.4
  154.9 0.7 copy-start.5
  155.6 0.7 copy-start.6
